TPU v7x, 32 devices: a whole 2x2x4 slice. The times are simulated.
32 devices in a mesh: pos: 2 (over core), rows: 16 (over z, y, x).
Axes of the slice: x: 2, y: 2, z: 4, core: 2. Of those that a mesh axis runs over, the one named last changes fastest.
Arguments:
- matrix: float32 [8192, 512], P('rows', 'pos'), may hold values from -40 to 40
- shifts: int32 [3], replicated, may hold values from 1 to 7, as said below
Outputs:
- rotated: float32 [8192, 512], P('rows', 'pos')
Inputs may be any that keep to these rules, and one draw needn't show every extreme that they name: `shifts`: each entry is a distance between pair positions, taken modulo 2; 7 and 1 both occur in every draw.
All inputs are finite; a program needn't handle non-finite values. Where the computation divides by a largest or mean magnitude, that divisor is 1e-20 or more.
Results may differ from a plain program's by a relative error of at most 0.00018.
Values sent between devices are 32-bit elements; how exact they have to be, the bound alone decides.
No kernel may reach another device: no remote copies, remote signals or barrier semaphores. Data moves between devices by JAX's collectives and lax.ppermute only.
A program may use at most 64 MiB of HBM per device.

v0:
```python
import jax
import jax.numpy as jnp
from jax import lax
from jax.sharding import PartitionSpec as P

ROUNDS = 3
NS_STEPS = 3


def from_behind(x, axis, by):
    size = lax.axis_size(axis)
    return lax.ppermute(x, axis, [(i, (i + by) % size) for i in range(size)])


def product(left, right):
    return jnp.dot(left, right, precision=lax.Precision.HIGHEST, preferred_element_type=jnp.float32)


def rotation(gram_matrix):
    width = gram_matrix.shape[0]
    identity = jnp.eye(width, dtype=gram_matrix.dtype)
    inverse_norm = 1.0 / jnp.sqrt(jnp.diagonal(gram_matrix) + 1e-06)
    scaled = gram_matrix * inverse_norm[:, None] * inverse_norm[None, :]
    upper = jnp.triu(scaled, 1)
    skew_raw = upper - upper.T
    bound_value = jnp.max(jnp.sum(jnp.abs(skew_raw), axis=1))
    skew = skew_raw / (1.0 + 2.0 * bound_value)
    shifted = identity - skew
    inverse = identity + skew
    for step in range(NS_STEPS):
        inverse = product(inverse, 2.0 * identity - product(shifted, inverse))
    return product(inverse, identity + skew)


def make_branch(step_size):

    def moved(block):
        if step_size == 0:
            return block
        return from_behind(block, "pos", step_size)

    return moved


def shards(matrix, shifts):
    current = matrix
    half = current.shape[1] // 2
    position_count = lax.axis_size("pos")
    for round_index in range(ROUNDS):
        gram_matrix = lax.psum(product(current.T, current), "rows")
        current = product(current, rotation(gram_matrix))
        distance = shifts[round_index] % position_count
        first_cols = current[:, :half]
        second_cols = current[:, half:]
        branches = [make_branch(step_size) for step_size in range(position_count)]
        second_cols = lax.switch(distance, branches, second_cols)
        current = jnp.concatenate([first_cols, second_cols], axis=1)
    return current


def solution(mesh):
    placed = (P("rows", "pos"), P())
    return jax.shard_map(
        shards, mesh=mesh, in_specs=placed, out_specs=P("rows", "pos"), check_vma=False
    )
```

profile of v0, /device:TPU:0, one launch (start us, length us, event | category | flops | bytes accessed | tf_op | source)
XLA Modules:
  0.0 374.8 jit_solution(13292800468868917064)
XLA Ops:
  6.5 1.0 copy-done
  7.6 1.7 fusion.15
  9.4 0.6 copy-done.4
  10.0 0.6 fusion.14
  12.3 0.1 copy.23
  12.5 0.2 copy.24
  12.7 109.5 %all-reduce.4.cloned.1.call-done = f32[256,256]{1,0:T(8,128)} async-done(((f32[256,256]{1,0:T(8,128)}), f32[256,256]{1,0:T(8,128)}) %all-reduce.4.cloned.1.call-update) | async-done | bytes 262160 | tf_op jit(solution)/shard_map/psum | solution.py:50
  122.2 2.6 gather_fusion
  124.8 0.1 multiply_select_fusion.2
  125.0 0.1 copy.26
  125.1 0.1 abs_reduce_fusion.2
  125.2 0.6 reduce_max.27
  126.5 0.6 convolution_subtract_fusion.8
  127.1 0.4 fusion.5
  127.6 0.6 convolution_subtract_fusion.7
  128.2 0.4 fusion.16
  128.6 0.6 convolution_subtract_fusion.6
  129.2 0.4 fusion.17
  129.6 0.4 fusion.4
  130.1 1.1 convolution_bitcast_fusion
  131.2 1.3 fusion.3
  132.6 0.2 all-reduce.8.cloned.1.call-start
  134.8 0.1 copy.32
  134.9 103.7 %all-reduce.6.cloned.1.call-done = f32[256,256]{0,1:T(8,128)} async-done(((f32[256,256]{0,1:T(8,128)}), f32[256,256]{0,1:T(8,128)}) %all-reduce.6.cloned.1.call-update) | async-done | bytes 262160 | tf_op jit(solution)/shard_map/psum | solution.py:50
  238.6 2.7 gather_fusion.1
  241.3 0.1 multiply_select_fusion.1
  241.4 0.1 copy.31
  241.5 0.1 abs_reduce_fusion.1
  241.6 0.6 reduce_max.28
  242.9 0.1 fusion.12
  243.0 0.4 convolution_subtract_fusion.5
  243.4 0.6 fusion.18
  244.0 0.6 convolution_subtract_fusion.4
  244.6 0.4 fusion.19
  245.1 0.6 convolution_subtract_fusion.3
  245.7 0.4 fusion.20
  246.1 0.4 fusion.21
  246.5 0.7 fusion.2
  247.2 1.9 conditional.4
  247.3 0.1 copy.35
  247.4 0.1 collective-permute-start.1
  247.5 1.5 collective-permute-done.1
  249.0 0.1 copy.48
  249.1 1.3 fusion.1
  252.3 104.2 %all-reduce.8.cloned.1.call-done = f32[256,256]{0,1:T(8,128)} async-done(((f32[256,256]{0,1:T(8,128)}), f32[256,256]{0,1:T(8,128)}) %all-reduce.8.cloned.1.call-update) | async-done | bytes 262160 | tf_op jit(solution)/shard_map/psum | solution.py:50
  356.5 2.7 gather_fusion.2
  359.2 0.1 multiply_select_fusion
  359.3 0.1 copy.38
  359.4 0.2 abs_reduce_fusion
  359.6 0.6 reduce_max.29
  360.9 0.1 broadcast_divide_fusion
  361.0 0.6 convolution_subtract_fusion.2
  361.6 0.4 fusion.7
  362.1 0.6 convolution_subtract_fusion.1
  362.7 0.4 fusion.22
  363.1 0.6 convolution_subtract_fusion
  363.7 0.4 fusion.23
  364.1 0.4 fusion.6
  364.6 0.7 fusion
  365.3 1.9 conditional.5
  365.3 0.1 copy.40
  365.5 1.5 collective-permute-done.2
  367.0 0.1 copy.50
  367.2 1.0 copy.42
  (30 shorter events, 0.5 us)
Async XLA Ops:
  6.5 1.0 copy-start
  6.5 115.6 %all-reduce.4.cloned.1.call-start = ((), (), s32[]{:S(2)}) async-start(), calls=%async_computation | async-start | bytes 524288 | tf_op jit(solution)/shard_map/psum | solution.py:50
  9.3 229.3 %all-reduce.6.cloned.1.call-start = ((), (), s32[]{:S(2)}) async-start(), calls=%async_computation.1 | async-start | bytes 524288 | tf_op jit(solution)/shard_map/psum | solution.py:50
  9.4 0.7 copy-start.4
  122.2 2.6 copy-start.3
  132.6 223.9 %all-reduce.8.cloned.1.call-start = ((), (), s32[]{:S(2)}) async-start(), calls=%async_computation.2 | async-start | bytes 524288 | tf_op jit(solution)/shard_map/psum | solution.py:50
  238.6 2.7 copy-start.1
  247.4 1.6 collective-permute-start.1
  356.5 2.7 copy-start.2
  365.4 1.6 collective-permute-start.2
Sparse Core Ops, SparseCore 0:
  12.6 109.5 all-reduce.3
  132.7 105.8 all-reduce.5
  250.6 105.8 all-reduce.7
where the time goes:
time: 375 us
  waiting for transfers between devices  320 us (85%)
  between operations  20.9 us (6%)
  matrix products  17.2 us (5%)
  local copies, waits for them, and re-layouts  12.7 us (3%)
    psum x3, waiting for transfers between devices, shards(): gram_matrix = lax.psum(product(current.T, current), 'rows')  317 us
    dot_general x27, matrix products, product(): jnp.dot(left, right, precision=lax.Precision.HIGHEST, preferred_element_t...  17.2 us
    gather x3, local copies, waits for them, and re-layouts, rotation(): inverse_norm = 1.0 / jnp.sqrt(jnp.diagonal(gram_matrix) + 1e-06)  7.96 us
  transfers between devices with their start and end apart: 5, of which 5 were waited for; matrix products, arithmetic and copies ran while one was open for 0% of the time, Pallas kernels for 0%

commit v1 on v0

--- a/solution.py
+++ b/solution.py
@@ -1,10 +1,19 @@
+import functools
+
 import jax
 import jax.numpy as jnp
 from jax import lax
+from jax.experimental import pallas as pl
+from jax.experimental.pallas import tpu as pltpu
 from jax.sharding import PartitionSpec as P
 
 ROUNDS = 3
 NS_STEPS = 3
+EXTRA = 8
+F32 = jnp.float32
+BF16 = jnp.bfloat16
+VMEM = pl.BlockSpec(memory_space=pltpu.VMEM)
+SMEM = pl.BlockSpec(memory_space=pltpu.SMEM)
 
 
 def from_behind(x, axis, by):
@@ -13,7 +22,7 @@
 
 
 def product(left, right):
-    return jnp.dot(left, right, precision=lax.Precision.HIGHEST, preferred_element_type=jnp.float32)
+    return jnp.dot(left, right, precision=lax.Precision.HIGHEST, preferred_element_type=F32)
 
 
 def rotation(gram_matrix):
@@ -58,8 +67,232 @@
     return current
 
 
+def split(x):
+    high = x.astype(BF16)
+    return high, (x - high.astype(F32)).astype(BF16)
+
+
+def dot(left, right, contract=1):
+    return lax.dot_general(
+        left, right, (((contract,), (0,)), ((), ())), preferred_element_type=F32
+    )
+
+
+def dot3(left, right, contract=1):
+    (left_high, left_low), (right_high, right_low) = left, right
+    return (
+        dot(left_high, right_low, contract)
+        + dot(left_low, right_high, contract)
+        + dot(left_high, right_high, contract)
+    )
+
+
+def gram_kernel(where, own, other, *refs):
+    outs, (high, low, blocks) = refs[:4], refs[4:]
+    half = own.shape[1] // 2
+    position, corner = where[0], where[1]
+    for ref, place in ((own, position), (other, 1 - position)):
+        part = split(ref[...])
+        high[place], low[place] = part
+    mine = high[position], low[position]
+    gram = dot3(mine, mine, 0)
+    columns = pl.ds(pl.multiple_of(position * half, half), half)
+    cross = dot3((high[0], low[0]), (high[1, :, columns], low[1, :, columns]), 0)
+    first, second = gram[:half, :half], gram[half:, half:]
+    row = lax.broadcasted_iota(jnp.int32, (half, half), 0)
+    col = lax.broadcasted_iota(jnp.int32, (half, half), 1)
+    blocks[0, :half] = jnp.where(col >= row, first, second)
+    diagonal = jnp.sum(jnp.where(col == row, second, 0.0), axis=0, keepdims=True)
+    blocks[0, half:] = jnp.broadcast_to(diagonal, (EXTRA, half))
+    blocks[1, :half] = gram[:half, half:]
+    blocks[2, :half] = cross[:half]
+    blocks[3, :half] = cross[half:]
+    for slot in (1, 2, 3):
+        blocks[slot, half:] = jnp.zeros((EXTRA, half), F32)
+    for offset, out in enumerate(outs):
+        out[...] = blocks[corner ^ offset]
+
+
+def sum_kernel(*refs):
+    ins, out = refs[:-1], refs[-1]
+    total = ins[0][...]
+    for ref in ins[1:]:
+        total = total + ref[...]
+    out[...] = total
+
+
+def symmetric(block, extra):
+    half = block.shape[0]
+    row = lax.broadcasted_iota(jnp.int32, (half, half), 0)
+    col = lax.broadcasted_iota(jnp.int32, (half, half), 1)
+    turned = block.T
+    first = jnp.where(col >= row, block, turned)
+    second = jnp.where(col > row, turned, jnp.where(col < row, block, extra[:1]))
+    return first, second
+
+
+def beside(left, right):
+    return jnp.concatenate([left, right], axis=1)
+
+
+def above(top, bottom):
+    return jnp.concatenate([top, bottom], axis=0)
+
+
+def cayley_of(gram):
+    width = gram.shape[0]
+    row = lax.broadcasted_iota(jnp.int32, (width, width), 0)
+    col = lax.broadcasted_iota(jnp.int32, (width, width), 1)
+    on_diagonal = row == col
+    diagonal = jnp.where(on_diagonal, gram, 0.0)
+    inverse_row = 1.0 / jnp.sqrt(jnp.sum(diagonal, axis=0, keepdims=True) + 1e-06)
+    inverse_col = 1.0 / jnp.sqrt(jnp.sum(diagonal, axis=1, keepdims=True) + 1e-06)
+    scaled = gram * inverse_col * inverse_row
+    raw = jnp.where(on_diagonal, 0.0, jnp.where(col > row, scaled, -scaled))
+    bound = jnp.max(jnp.sum(jnp.abs(raw), axis=0, keepdims=True), axis=1, keepdims=True)
+    skew = raw / (1.0 + 2.0 * bound)
+    identity = jnp.where(on_diagonal, 1.0, 0.0)
+    skew_parts = split(skew)
+    square = dot3(skew_parts, skew_parts)
+    square_parts = split(square)
+    cube = dot3(skew_parts, square_parts)
+    fourth = dot3(square_parts, square_parts)
+    fourth_parts = split(fourth)
+    base = identity + 2.0 * (skew + square + cube) + fourth
+    eighth = dot(fourth_parts[0], fourth_parts[0])
+    base = base + dot3(split(base), fourth_parts)
+    return base + dot(base.astype(BF16), eighth.astype(BF16))
+
+
+def rounds_kernel(scalars, *refs):
+    mine, theirs, (own, other), out = refs[:4], refs[4:8], refs[8:10], refs[10]
+    pieces, high, low, turn_high, turn_low = refs[11:]
+    position, corner = scalars[0], scalars[1]
+    half = own.shape[1] // 2
+    for refs_of, place in ((mine, position), (theirs, 1 - position)):
+        for offset, ref in enumerate(refs_of):
+            pieces[place, corner ^ offset] = ref[...]
+    for ref, place in ((own, position), (other, 1 - position)):
+        for side in range(2):
+            part = split(ref[:, side * half : (side + 1) * half])
+            high[side, place], low[side, place] = part
+    grams = []
+    for place in range(2):
+        first, second = symmetric(pieces[place, 0, :half], pieces[place, 0, half:])
+        between = pieces[place, 1, :half]
+        grams.append([[first, between], [between.T, second]])
+    cross = [
+        [pieces[0, 2, :half], pieces[1, 2, :half]],
+        [pieces[0, 3, :half], pieces[1, 3, :half]],
+    ]
+    for step in range(ROUNDS):
+        odd = scalars[2 + step] % 2
+        turns = []
+        for place in range(2):
+            (aa, ab), (ba, bb) = grams[place]
+            turns.append(split(cayley_of(above(beside(aa, ab), beside(ba, bb)))))
+        if step == ROUNDS - 1:
+            for place in range(2):
+                turn_high[place], turn_low[place] = turns[place]
+            for side, place in ((0, position), (1, (position + odd) % 2)):
+                held = tuple(beside(x[0, place], x[1, place]) for x in (high, low))
+                cols = slice(side * half, (side + 1) * half)
+                turn = turn_high[place, :, cols], turn_low[place, :, cols]
+                out[:, cols] = dot3(held, turn)
+            break
+        moved = []
+        for place in range(2):
+            held = tuple(beside(x[0, place], x[1, place]) for x in (high, low))
+            moved.append(dot3(held, turns[place]))
+        for place in range(2):
+            high[0, place], low[0, place] = split(moved[place][:, :half])
+            to = (place + odd) % 2
+            high[1, to], low[1, to] = split(moved[place][:, half:])
+        new_grams = []
+        for place in range(2):
+            (aa, ab), (ba, bb) = grams[place]
+            gram = above(beside(aa, ab), beside(ba, bb))
+            right = dot3(split(gram), turns[place])
+            gram = dot3(turns[place], split(right), 0)
+            new_grams.append(gram)
+        (aa, ab), (ba, bb) = cross
+        right = dot3(split(above(beside(aa, ab), beside(ba, bb))), turns[1])
+        between = dot3(turns[0], split(right), 0)
+        zero, one = new_grams
+        swap = odd == 1
+        quarters = lambda x: ((x[:half, :half], x[:half, half:]), (x[half:, :half], x[half:, half:]))
+        (z_aa, z_ab), (z_ba, z_bb) = quarters(zero)
+        (o_aa, o_ab), (o_ba, o_bb) = quarters(one)
+        (c_aa, c_ab), (c_ba, c_bb) = quarters(between)
+        pick = functools.partial(jnp.where, swap)
+        grams = [
+            [[z_aa, pick(c_ab, z_ab)], [pick(c_ab.T, z_ba), pick(o_bb, z_bb)]],
+            [[o_aa, pick(c_ba.T, o_ab)], [pick(c_ba, o_ba), pick(z_bb, o_bb)]],
+        ]
+        cross = [[c_aa, pick(z_ab, c_ab)], [pick(o_ba, c_ba), pick(c_bb.T, c_bb)]]
+
+
+def kernel_of(body, out_shape, ins, scratch=()):
+    return pl.pallas_call(
+        body,
+        out_shape=out_shape,
+        in_specs=ins,
+        out_specs=jax.tree.map(lambda _: VMEM, out_shape),
+        scratch_shapes=list(scratch),
+        compiler_params=pltpu.CompilerParams(vmem_limit_bytes=40 * 2**20),
+    )
+
+
+def across(x, mask):
+    size = lax.axis_size("rows")
+    return lax.ppermute(x, "rows", [(i, i ^ mask) for i in range(size)])
+
+
+def one_sum(matrix, shifts):
+    rows, width = matrix.shape
+    half = width // 2
+    piece = jax.ShapeDtypeStruct((half + EXTRA, half), F32)
+    size = lax.axis_size("rows")
+    position = lax.axis_index("pos")
+    corner = lax.axis_index("rows") % 4
+    where = jnp.stack([position, corner]).astype(jnp.int32)
+    other = lax.ppermute(matrix, "pos", [(0, 1), (1, 0)])
+    pieces = kernel_of(
+        gram_kernel,
+        [piece] * 4,
+        [SMEM, VMEM, VMEM],
+        [
+            pltpu.VMEM((2, rows, width), BF16),
+            pltpu.VMEM((2, rows, width), BF16),
+            pltpu.VMEM((4, half + EXTRA, half), F32),
+        ],
+    )(where, matrix, other)
+
+    def total(*arrays):
+        return kernel_of(sum_kernel, piece, [VMEM] * len(arrays))(*arrays)
+
+    held = total(pieces[0], *[across(pieces[mask], mask) for mask in (1, 2, 3)])
+    held = total(held, *[across(held, mask) for mask in range(4, size, 4)])
+    mine = [held] + [across(held, mask) for mask in (1, 2, 3)]
+    theirs = [lax.ppermute(x, "pos", [(0, 1), (1, 0)]) for x in mine]
+    scalars = jnp.concatenate([where, shifts])
+    return kernel_of(
+        rounds_kernel,
+        jax.ShapeDtypeStruct((rows, width), F32),
+        [SMEM] + [VMEM] * 10,
+        [
+            pltpu.VMEM((2, 4, half + EXTRA, half), F32),
+            pltpu.VMEM((2, 2, rows, half), BF16),
+            pltpu.VMEM((2, 2, rows, half), BF16),
+            pltpu.VMEM((2, width, width), BF16),
+            pltpu.VMEM((2, width, width), BF16),
+        ],
+    )(scalars, *mine, *theirs, matrix, other)
+
+
 def solution(mesh):
     placed = (P("rows", "pos"), P())
+    plan = one_sum if mesh.shape["pos"] == 2 and mesh.shape["rows"] == 16 else shards
     return jax.shard_map(
-        shards, mesh=mesh, in_specs=placed, out_specs=P("rows", "pos"), check_vma=False
-    )
+        plan, mesh=mesh, in_specs=placed, out_specs=P("rows", "pos"), check_vma=False
+    )

time: 375 us -> 43.4 us (0.12)
  waiting for transfers between devices: 320 us -> 15.1 us
  between operations: 20.9 us -> 0.04 us
  matrix products: 17.2 us -> 0 us
  Pallas kernels: 0 us -> 13.8 us
  starting transfers between devices: 0.41 us -> 13.1 us
  local copies, waits for them, and re-layouts: 12.7 us -> 1.05 us
    psum x3 -> x0, waiting for transfers between devices: 317 us -> none  [shards(): gram_matrix = lax.psum(product(current.T, current), 'rows')]
    dot_general x27 -> x0, matrix products: 17.2 us -> none  [product(): jnp.dot(left, right, precision=lax.Precision.HIGHEST, preferred_element_t...]
    pallas_call x0 -> x4, Pallas kernels: none -> 13.8 us  [the longest x1 12.3 us: one_sum(): kernel_of(rounds_kernel, jax.ShapeDtypeStruct((rows, width), F32), [SMEM]...]
    ppermute x2 -> x14, starting transfers between devices: 0.14 us -> 13.1 us  [the longest x9 12.5 us: across(): return lax.ppermute(x, 'rows', [(i, i ^ mask) for i in range(size)])]
    ppermute x2 -> x14, waiting for transfers between devices: 3.04 us -> 15.1 us  [the longest x9 12.3 us: across(): return lax.ppermute(x, 'rows', [(i, i ^ mask) for i in range(size)])]
    gather x3 -> x0, local copies, waits for them, and re-layouts: 7.96 us -> none  [rotation(): inverse_norm = 1.0 / jnp.sqrt(jnp.diagonal(gram_matrix) + 1e-06)]
  transfers between devices with their start and end apart: 5 -> 14, of which waited for: 5 -> 12; matrix products, arithmetic and copies ran while one was open for 0% -> 0% of each run, Pallas kernels for 0% -> 0%
where the time goes in v1:
time: 43.4 us; the launch traced here: 43.3 us
  waiting for transfers between devices  15.1 us (35%)
  Pallas kernels  13.8 us (32%)
  starting transfers between devices  13.1 us (30%)
  local copies, waits for them, and re-layouts  1.05 us (2%)
    ppermute x9, starting transfers between devices, across(): return lax.ppermute(x, 'rows', [(i, i ^ mask) for i in range(size)])  12.5 us
    pallas_call x1, Pallas kernels, one_sum(): kernel_of(rounds_kernel, jax.ShapeDtypeStruct((rows, width), F32), [SMEM]...  12.3 us
    ppermute x9, waiting for transfers between devices, across(): return lax.ppermute(x, 'rows', [(i, i ^ mask) for i in range(size)])  12.3 us
    ppermute x1, waiting for transfers between devices, one_sum(): other = lax.ppermute(matrix, 'pos', [(0, 1), (1, 0)])  1.67 us
    pallas_call x1, Pallas kernels, one_sum(): kernel_of(gram_kernel, [piece] * 4, [SMEM, VMEM, VMEM], [pltpu.VMEM((2, r...  1.41 us
    ppermute x4, waiting for transfers between devices, one_sum(): theirs = [lax.ppermute(x, 'pos', [(0, 1), (1, 0)]) for x in mine]  1.18 us
    unnamed x6, local copies, waits for them, and re-layouts  1.05 us
  transfers between devices with their start and end apart: 14, of which 12 were waited for; matrix products, arithmetic and copies ran while one was open for 0% of the time, Pallas kernels for 0%

profile of v1, /device:TPU:0, one launch (start us, length us, event | category | flops | bytes accessed | tf_op | source)
XLA Modules:
  0.0 43.3 jit_solution(3218528023941127943)
XLA Ops:
  0.0 0.5 %collective-permute-start = (f32[512,256]{1,0:T(8,128)}, f32[512,256]{1,0:T(8,128)S(1)}, u32[]{:S(2)}, u32[]{:S(2)}) collective-permute-start(f32[512,256]{1,0:T(8,128)} %refs_8_.1), channel_id=1, source_target_pairs={{0,16},{16,0},{1,17},{17,1},{2,18},{18,2},{3,19},{19,3},{4,20},{20... | collective-permute-start | bytes 1572872 | tf_op jit(solution)/shard_map/ppermute | solution.py:259
  0.5 0.1 pad_add_fusion.1.where
  0.5 1.7 %collective-permute-done.other.refs_9_ = f32[512,256]{1,0:T(8,128)S(1)} collective-permute-done((f32[512,256]{1,0:T(8,128)}, f32[512,256]{1,0:T(8,128)S(1)}, u32[]{:S(2)}, u32[]{:S(2)}) %collective-permute-start) | collective-permute-done | bytes 524320 | tf_op jit(solution)/shard_map/ppermute | solution.py:259
  2.2 0.0 copy-start
  2.2 1.0 %copy-done = f32[512,256]{1,0:T(8,128)S(1)} copy-done((f32[512,256]{1,0:T(8,128)S(1)}, f32[512,256]{1,0:T(8,128)}, u32[]{:S(2)}) %copy-start) | copy-done | bytes 524312
  3.2 1.4 %shard_map.28 = (f32[136,128]{1,0:T(8,128)S(1)}, f32[136,128]{1,0:T(8,128)S(1)}, f32[136,128]{1,0:T(8,128)S(1)}, f32[136,128]{1,0:T(8,128)S(1)}) custom-call(s32[2]{0:T(128)S(1)} %pad_add_fusion.1.where, f32[512,256]{1,0:T(8,128)S(1)} %copy-done, f32[512,256]{1,0:T(8,128)S(1)} %collective-permute-done.other.refs_9_), custom_call_target="tpu_custom_call" | custom-call | tf_op jit(solution)/shard_map/pallas_call | solution.py:260
  4.7 0.0 copy-start.1
  4.7 2.9 %collective-permute-start.1 = (f32[136,128]{1,0:T(8,128)S(1)}, f32[136,128]{1,0:T(8,128)S(1)}, u32[]{:S(2)}, u32[]{:S(2)}) collective-permute-start(f32[136,128]{1,0:T(8,128)S(1)} %get-tuple-element.10), channel_id=1, source_target_pairs={{0,1},{1,0},{2,3},{3,2},{4,5},{5,4},{6,7},{7,6},{8,9},{9,8},{10,11... | collective-permute-start | bytes 208904 | tf_op jit(solution)/shard_map/ppermute | solution.py:248
  7.6 1.5 %collective-permute-start.2 = (f32[136,128]{1,0:T(8,128)S(1)}, f32[136,128]{1,0:T(8,128)S(1)}, u32[]{:S(2)}, u32[]{:S(2)}) collective-permute-start(f32[136,128]{1,0:T(8,128)S(1)} %get-tuple-element.11), channel_id=1, source_target_pairs={{0,2},{1,3},{2,0},{3,1},{4,6},{5,7},{6,4},{7,5},{8,10},{9,11},{10,... | collective-permute-start | bytes 208904 | tf_op jit(solution)/shard_map/ppermute | solution.py:248
  9.1 0.0 collective-permute-start.3
  9.1 0.9 %collective-permute-done.1.refs_1_ = f32[136,128]{1,0:T(8,128)S(1)} collective-permute-done((f32[136,128]{1,0:T(8,128)S(1)}, f32[136,128]{1,0:T(8,128)S(1)}, u32[]{:S(2)}, u32[]{:S(2)}) %collective-permute-start.1) | collective-permute-done | bytes 69664 | tf_op jit(solution)/shard_map/ppermute | solution.py:248
  10.1 1.8 %collective-permute-done.2.refs_2_ = f32[136,128]{1,0:T(8,128)S(1)} collective-permute-done((f32[136,128]{1,0:T(8,128)S(1)}, f32[136,128]{1,0:T(8,128)S(1)}, u32[]{:S(2)}, u32[]{:S(2)}) %collective-permute-start.2) | collective-permute-done | bytes 69664 | tf_op jit(solution)/shard_map/ppermute | solution.py:248
  11.9 2.4 %collective-permute-done.3.refs_3_ = f32[136,128]{1,0:T(8,128)S(1)} collective-permute-done((f32[136,128]{1,0:T(8,128)S(1)}, f32[136,128]{1,0:T(8,128)S(1)}, u32[]{:S(2)}, u32[]{:S(2)}) %collective-permute-start.3) | collective-permute-done | bytes 69664 | tf_op jit(solution)/shard_map/ppermute | solution.py:248
  14.3 0.0 copy-start.2
  14.4 3.7 %collective-permute-start.6 = (f32[136,128]{1,0:T(8,128)S(1)}, f32[136,128]{1,0:T(8,128)S(1)}, u32[]{:S(2)}, u32[]{:S(2)}) collective-permute-start(f32[136,128]{1,0:T(8,128)S(1)} %shard_map.29.refs_0_), channel_id=1, source_target_pairs={{0,12},{1,13},{2,14},{3,15},{4,8},{5,9},{6,10},{7,11},{8,4},{9,5},... | collective-permute-start | bytes 208904 | tf_op jit(solution)/shard_map/ppermute | solution.py:248
  18.0 0.0 collective-permute-start.5
  18.0 0.8 %collective-permute-start.4 = (f32[136,128]{1,0:T(8,128)S(1)}, f32[136,128]{1,0:T(8,128)S(1)}, u32[]{:S(2)}, u32[]{:S(2)}) collective-permute-start(f32[136,128]{1,0:T(8,128)S(1)} %shard_map.29.refs_0_), channel_id=1, source_target_pairs={{0,4},{1,5},{2,6},{3,7},{4,0},{5,1},{6,2},{7,3},{8,12},{9,13},{10,... | collective-permute-start | bytes 208904 | tf_op jit(solution)/shard_map/ppermute | solution.py:248
  18.8 1.7 %collective-permute-done.6.refs_3_ = f32[136,128]{1,0:T(8,128)S(1)} collective-permute-done((f32[136,128]{1,0:T(8,128)S(1)}, f32[136,128]{1,0:T(8,128)S(1)}, u32[]{:S(2)}, u32[]{:S(2)}) %collective-permute-start.6) | collective-permute-done | bytes 69664 | tf_op jit(solution)/shard_map/ppermute | solution.py:248
  20.5 2.7 %collective-permute-done.5.refs_2_ = f32[136,128]{1,0:T(8,128)S(1)} collective-permute-done((f32[136,128]{1,0:T(8,128)S(1)}, f32[136,128]{1,0:T(8,128)S(1)}, u32[]{:S(2)}, u32[]{:S(2)}) %collective-permute-start.5) | collective-permute-done | bytes 69664 | tf_op jit(solution)/shard_map/ppermute | solution.py:248
  23.2 0.0 collective-permute-done.4.refs_1_
  23.3 0.6 %collective-permute-start.9 = (f32[136,128]{1,0:T(8,128)S(1)}, f32[136,128]{1,0:T(8,128)S(1)}, u32[]{:S(2)}, u32[]{:S(2)}) collective-permute-start(f32[136,128]{1,0:T(8,128)S(1)} %shard_map.30.refs_0_), channel_id=1, source_target_pairs={{0,3},{1,2},{2,1},{3,0},{4,7},{5,6},{6,5},{7,4},{8,11},{9,10},{10,... | collective-permute-start | bytes 208904 | tf_op jit(solution)/shard_map/ppermute | solution.py:248
  23.9 1.5 %collective-permute-start.8 = (f32[136,128]{1,0:T(8,128)S(1)}, f32[136,128]{1,0:T(8,128)S(1)}, u32[]{:S(2)}, u32[]{:S(2)}) collective-permute-start(f32[136,128]{1,0:T(8,128)S(1)} %shard_map.30.refs_0_), channel_id=1, source_target_pairs={{0,2},{1,3},{2,0},{3,1},{4,6},{5,7},{6,4},{7,5},{8,10},{9,11},{10,... | collective-permute-start | bytes 208904 | tf_op jit(solution)/shard_map/ppermute | solution.py:248
  25.4 1.4 %collective-permute-start.7 = (f32[136,128]{1,0:T(8,128)S(1)}, f32[136,128]{1,0:T(8,128)S(1)}, u32[]{:S(2)}, u32[]{:S(2)}) collective-permute-start(f32[136,128]{1,0:T(8,128)S(1)} %shard_map.30.refs_0_), channel_id=1, source_target_pairs={{0,1},{1,0},{2,3},{3,2},{4,5},{5,4},{6,7},{7,6},{8,9},{9,8},{10,11... | collective-permute-start | bytes 208904 | tf_op jit(solution)/shard_map/ppermute | solution.py:248
  26.8 0.0 collective-permute-start.10
  26.8 1.8 %collective-permute-done.9.refs_3_ = f32[136,128]{1,0:T(8,128)S(1)} collective-permute-done((f32[136,128]{1,0:T(8,128)S(1)}, f32[136,128]{1,0:T(8,128)S(1)}, u32[]{:S(2)}, u32[]{:S(2)}) %collective-permute-start.9) | collective-permute-done | bytes 69664 | tf_op jit(solution)/shard_map/ppermute | solution.py:248
  28.6 0.0 collective-permute-start.13
  28.6 0.3 collective-permute-done.8.refs_2_
  29.0 0.2 collective-permute-start.12
  29.2 0.5 %collective-permute-done.7.refs_1_ = f32[136,128]{1,0:T(8,128)S(1)} collective-permute-done((f32[136,128]{1,0:T(8,128)S(1)}, f32[136,128]{1,0:T(8,128)S(1)}, u32[]{:S(2)}, u32[]{:S(2)}) %collective-permute-start.7) | collective-permute-done | bytes 69664 | tf_op jit(solution)/shard_map/ppermute | solution.py:248
  29.7 0.0 collective-permute-start.11
  29.7 0.0 copy-done.2
  29.7 0.1 pad_add_fusion.scalars
  29.8 0.0 collective-permute-done.10.refs_4_
  29.8 0.1 collective-permute-done.13.refs_7_
  29.9 0.3 collective-permute-done.12.refs_6_
  30.2 0.7 %collective-permute-done.11.refs_5_ = f32[136,128]{1,0:T(8,128)S(1)} collective-permute-done((f32[136,128]{1,0:T(8,128)S(1)}, f32[136,128]{1,0:T(8,128)S(1)}, u32[]{:S(2)}, u32[]{:S(2)}) %collective-permute-start.11) | collective-permute-done | bytes 69664 | tf_op jit(solution)/shard_map/ppermute | solution.py:277
  30.9 0.0 copy-done.1
  31.0 12.3 %shard_map.31 = f32[512,256]{1,0:T(8,128)} custom-call(s32[5]{0:T(128)S(1)} %pad_add_fusion.scalars, f32[136,128]{1,0:T(8,128)S(1)} %shard_map.30.refs_0_, f32[136,128]{1,0:T(8,128)S(1)} %collective-permute-done.7.refs_1_, f32[136,128]{1,0:T(8,128)S(1)} %collective-permute-done.8.refs_2_, f32[136,128]{1,0:T(8,128)S(1)} %collective-permute-done.9.refs_3_, ...), custom_call_target="tpu_custom_call" | custom-call | tf_op jit(solution)/shard_map/pallas_call | solution.py:279
  (2 shorter events, 0.1 us)
Async XLA Ops:
  0.0 2.2 %collective-permute-start = (f32[512,256]{1,0:T(8,128)}, f32[512,256]{1,0:T(8,128)S(1)}, u32[]{:S(2)}, u32[]{:S(2)}) collective-permute-start(f32[512,256]{1,0:T(8,128)} %refs_8_.1), channel_id=1, source_target_pairs={{0,16},{16,0},{1,17},{17,1},{2,18},{18,2},{3,19},{19,3},{4,20},{20... | collective-permute-start | bytes 1572872 | tf_op jit(solution)/shard_map/ppermute | solution.py:259
  2.2 1.0 %copy-start = (f32[512,256]{1,0:T(8,128)S(1)}, f32[512,256]{1,0:T(8,128)}, u32[]{:S(2)}) copy-start(f32[512,256]{1,0:T(8,128)} %refs_8_.1) | copy-start | bytes 1572868
  4.7 26.3 %copy-start.1 = (f32[512,256]{1,0:T(8,128)S(1)}, f32[512,256]{1,0:T(8,128)}, u32[]{:S(2)}) copy-start(f32[512,256]{1,0:T(8,128)} %refs_8_.1) | copy-start | bytes 1572868
  4.7 5.4 %collective-permute-start.1 = (f32[136,128]{1,0:T(8,128)S(1)}, f32[136,128]{1,0:T(8,128)S(1)}, u32[]{:S(2)}, u32[]{:S(2)}) collective-permute-start(f32[136,128]{1,0:T(8,128)S(1)} %get-tuple-element.10), channel_id=1, source_target_pairs={{0,1},{1,0},{2,3},{3,2},{4,5},{5,4},{6,7},{7,6},{8,9},{9,8},{10,11... | collective-permute-start | bytes 208904 | tf_op jit(solution)/shard_map/ppermute | solution.py:248
  7.6 4.3 %collective-permute-start.2 = (f32[136,128]{1,0:T(8,128)S(1)}, f32[136,128]{1,0:T(8,128)S(1)}, u32[]{:S(2)}, u32[]{:S(2)}) collective-permute-start(f32[136,128]{1,0:T(8,128)S(1)} %get-tuple-element.11), channel_id=1, source_target_pairs={{0,2},{1,3},{2,0},{3,1},{4,6},{5,7},{6,4},{7,5},{8,10},{9,11},{10,... | collective-permute-start | bytes 208904 | tf_op jit(solution)/shard_map/ppermute | solution.py:248
  9.1 5.2 %collective-permute-start.3 = (f32[136,128]{1,0:T(8,128)S(1)}, f32[136,128]{1,0:T(8,128)S(1)}, u32[]{:S(2)}, u32[]{:S(2)}) collective-permute-start(f32[136,128]{1,0:T(8,128)S(1)} %get-tuple-element.12), channel_id=1, source_target_pairs={{0,3},{1,2},{2,1},{3,0},{4,7},{5,6},{6,5},{7,4},{8,11},{9,10},{10,... | collective-permute-start | bytes 208904 | tf_op jit(solution)/shard_map/ppermute | solution.py:248
  14.3 15.3 %copy-start.2 = (s32[3]{0:T(128)S(1)}, s32[3]{0:T(128)}, u32[]{:S(2)}) copy-start(s32[3]{0:T(128)} %param.3) | copy-start | bytes 40
  14.4 6.2 %collective-permute-start.6 = (f32[136,128]{1,0:T(8,128)S(1)}, f32[136,128]{1,0:T(8,128)S(1)}, u32[]{:S(2)}, u32[]{:S(2)}) collective-permute-start(f32[136,128]{1,0:T(8,128)S(1)} %shard_map.29.refs_0_), channel_id=1, source_target_pairs={{0,12},{1,13},{2,14},{3,15},{4,8},{5,9},{6,10},{7,11},{8,4},{9,5},... | collective-permute-start | bytes 208904 | tf_op jit(solution)/shard_map/ppermute | solution.py:248
  18.0 5.2 %collective-permute-start.5 = (f32[136,128]{1,0:T(8,128)S(1)}, f32[136,128]{1,0:T(8,128)S(1)}, u32[]{:S(2)}, u32[]{:S(2)}) collective-permute-start(f32[136,128]{1,0:T(8,128)S(1)} %shard_map.29.refs_0_), channel_id=1, source_target_pairs={{0,8},{1,9},{2,10},{3,11},{4,12},{5,13},{6,14},{7,15},{8,0},{9,1},... | collective-permute-start | bytes 208904 | tf_op jit(solution)/shard_map/ppermute | solution.py:248
  18.0 5.2 %collective-permute-start.4 = (f32[136,128]{1,0:T(8,128)S(1)}, f32[136,128]{1,0:T(8,128)S(1)}, u32[]{:S(2)}, u32[]{:S(2)}) collective-permute-start(f32[136,128]{1,0:T(8,128)S(1)} %shard_map.29.refs_0_), channel_id=1, source_target_pairs={{0,4},{1,5},{2,6},{3,7},{4,0},{5,1},{6,2},{7,3},{8,12},{9,13},{10,... | collective-permute-start | bytes 208904 | tf_op jit(solution)/shard_map/ppermute | solution.py:248
  23.3 5.4 %collective-permute-start.9 = (f32[136,128]{1,0:T(8,128)S(1)}, f32[136,128]{1,0:T(8,128)S(1)}, u32[]{:S(2)}, u32[]{:S(2)}) collective-permute-start(f32[136,128]{1,0:T(8,128)S(1)} %shard_map.30.refs_0_), channel_id=1, source_target_pairs={{0,3},{1,2},{2,1},{3,0},{4,7},{5,6},{6,5},{7,4},{8,11},{9,10},{10,... | collective-permute-start | bytes 208904 | tf_op jit(solution)/shard_map/ppermute | solution.py:248
  23.9 5.1 %collective-permute-start.8 = (f32[136,128]{1,0:T(8,128)S(1)}, f32[136,128]{1,0:T(8,128)S(1)}, u32[]{:S(2)}, u32[]{:S(2)}) collective-permute-start(f32[136,128]{1,0:T(8,128)S(1)} %shard_map.30.refs_0_), channel_id=1, source_target_pairs={{0,2},{1,3},{2,0},{3,1},{4,6},{5,7},{6,4},{7,5},{8,10},{9,11},{10,... | collective-permute-start | bytes 208904 | tf_op jit(solution)/shard_map/ppermute | solution.py:248
  25.4 4.3 %collective-permute-start.7 = (f32[136,128]{1,0:T(8,128)S(1)}, f32[136,128]{1,0:T(8,128)S(1)}, u32[]{:S(2)}, u32[]{:S(2)}) collective-permute-start(f32[136,128]{1,0:T(8,128)S(1)} %shard_map.30.refs_0_), channel_id=1, source_target_pairs={{0,1},{1,0},{2,3},{3,2},{4,5},{5,4},{6,7},{7,6},{8,9},{9,8},{10,11... | collective-permute-start | bytes 208904 | tf_op jit(solution)/shard_map/ppermute | solution.py:248
  26.8 3.0 %collective-permute-start.10 = (f32[136,128]{1,0:T(8,128)S(1)}, f32[136,128]{1,0:T(8,128)S(1)}, u32[]{:S(2)}, u32[]{:S(2)}) collective-permute-start(f32[136,128]{1,0:T(8,128)S(1)} %shard_map.30.refs_0_), channel_id=1, source_target_pairs={{0,16},{16,0},{1,17},{17,1},{2,18},{18,2},{3,19},{19,3},{4,20},{20... | collective-permute-start | bytes 208904 | tf_op jit(solution)/shard_map/ppermute | solution.py:277
  28.6 1.3 %collective-permute-start.13 = (f32[136,128]{1,0:T(8,128)S(1)}, f32[136,128]{1,0:T(8,128)S(1)}, u32[]{:S(2)}, u32[]{:S(2)}) collective-permute-start(f32[136,128]{1,0:T(8,128)S(1)} %collective-permute-done.9.refs_3_), channel_id=1, source_target_pairs={{0,16},{16,0},{1,17},{17,1},{2,18},{18,2},{3,19},{19,3},{4,20},{20... | collective-permute-start | bytes 208904 | tf_op jit(solution)/shard_map/ppermute | solution.py:277
  29.0 1.3 %collective-permute-start.12 = (f32[136,128]{1,0:T(8,128)S(1)}, f32[136,128]{1,0:T(8,128)S(1)}, u32[]{:S(2)}, u32[]{:S(2)}) collective-permute-start(f32[136,128]{1,0:T(8,128)S(1)} %collective-permute-done.8.refs_2_), channel_id=1, source_target_pairs={{0,16},{16,0},{1,17},{17,1},{2,18},{18,2},{3,19},{19,3},{4,20},{20... | collective-permute-start | bytes 208904 | tf_op jit(solution)/shard_map/ppermute | solution.py:277
  29.7 1.3 %collective-permute-start.11 = (f32[136,128]{1,0:T(8,128)S(1)}, f32[136,128]{1,0:T(8,128)S(1)}, u32[]{:S(2)}, u32[]{:S(2)}) collective-permute-start(f32[136,128]{1,0:T(8,128)S(1)} %collective-permute-done.7.refs_1_), channel_id=1, source_target_pairs={{0,16},{16,0},{1,17},{17,1},{2,18},{18,2},{3,19},{19,3},{4,20},{20... | collective-permute-start | bytes 208904 | tf_op jit(solution)/shard_map/ppermute | solution.py:277

commit v2 on v1

v2 whole, which is shorter than its diff:
```python
import functools

import jax
import jax.numpy as jnp
from jax import lax
from jax.experimental import pallas as pl
from jax.experimental.pallas import tpu as pltpu
from jax.sharding import PartitionSpec as P

ROUNDS = 3
NS_STEPS = 3
EXTRA = 8
CHUNKS = 2
F32 = jnp.float32
BF16 = jnp.bfloat16
VMEM = pl.BlockSpec(memory_space=pltpu.VMEM)
HBM = pl.BlockSpec(memory_space=pltpu.HBM)


def from_behind(x, axis, by):
    size = lax.axis_size(axis)
    return lax.ppermute(x, axis, [(i, (i + by) % size) for i in range(size)])


def product(left, right):
    return jnp.dot(left, right, precision=lax.Precision.HIGHEST, preferred_element_type=F32)


def rotation(gram_matrix):
    width = gram_matrix.shape[0]
    identity = jnp.eye(width, dtype=gram_matrix.dtype)
    inverse_norm = 1.0 / jnp.sqrt(jnp.diagonal(gram_matrix) + 1e-06)
    scaled = gram_matrix * inverse_norm[:, None] * inverse_norm[None, :]
    upper = jnp.triu(scaled, 1)
    skew_raw = upper - upper.T
    bound_value = jnp.max(jnp.sum(jnp.abs(skew_raw), axis=1))
    skew = skew_raw / (1.0 + 2.0 * bound_value)
    shifted = identity - skew
    inverse = identity + skew
    for step in range(NS_STEPS):
        inverse = product(inverse, 2.0 * identity - product(shifted, inverse))
    return product(inverse, identity + skew)


def make_branch(step_size):

    def moved(block):
        if step_size == 0:
            return block
        return from_behind(block, "pos", step_size)

    return moved


def shards(matrix, shifts):
    current = matrix
    half = current.shape[1] // 2
    position_count = lax.axis_size("pos")
    for round_index in range(ROUNDS):
        gram_matrix = lax.psum(product(current.T, current), "rows")
        current = product(current, rotation(gram_matrix))
        distance = shifts[round_index] % position_count
        first_cols = current[:, :half]
        second_cols = current[:, half:]
        branches = [make_branch(step_size) for step_size in range(position_count)]
        second_cols = lax.switch(distance, branches, second_cols)
        current = jnp.concatenate([first_cols, second_cols], axis=1)
    return current


def split(x):
    high = x.astype(BF16)
    return high, (x - high.astype(F32)).astype(BF16)


def dot(left, right, contract=1):
    return lax.dot_general(
        left, right, (((contract,), (0,)), ((), ())), preferred_element_type=F32
    )


def dot3(left, right, contract=1):
    (left_high, left_low), (right_high, right_low) = left, right
    return (
        dot(left_high, right_low, contract)
        + dot(left_low, right_high, contract)
        + dot(left_high, right_high, contract)
    )


def own_kernel(own, high, low, gram, landed, arrived):
    span = own.shape[0] // CHUNKS
    copies = []
    for chunk in range(CHUNKS):
        rows = slice(chunk * span, (chunk + 1) * span)
        copies.append(pltpu.make_async_copy(own.at[rows], landed.at[rows], arrived.at[chunk]))
        copies[-1].start()
    total = None
    for chunk, copy in enumerate(copies):
        rows = slice(chunk * span, (chunk + 1) * span)
        copy.wait()
        parts = split(landed[rows])
        high[rows], low[rows] = parts
        part = dot3(parts, parts, 0)
        total = part if total is None else total + part
    gram[...] = total


def packed(gram):
    half = gram.shape[0] // 2
    first, second = gram[:half, :half], gram[half:, half:]
    row = lax.broadcasted_iota(jnp.int32, (half, half), 0)
    col = lax.broadcasted_iota(jnp.int32, (half, half), 1)
    diagonal = jnp.sum(jnp.where(col == row, second, 0.0), axis=0, keepdims=True)
    return jnp.where(col >= row, first, second), diagonal


def gram_kernel(other, own_high, own_low, own_gram, *refs):
    outs, (high, low, pieces) = refs[:4], refs[4:]
    position = lax.axis_index("pos")
    corner = lax.axis_index("rows") % 4
    half = other.shape[1] // 2
    high[...], low[...] = split(other[...])
    cross = dot3((own_high[...], own_low[...]), (high[...], low[...]), 0)
    first = position == 0
    gram = own_gram[...]
    square, diagonal = packed(gram)
    pieces[0, :half] = square
    pieces[0, half:] = jnp.broadcast_to(diagonal, (EXTRA, half))
    pieces[1, :half] = gram[:half, half:]
    pieces[2, :half] = jnp.where(first, cross[:half, :half], cross[half:, :half])
    pieces[3, :half] = jnp.where(first, cross[half:, :half], cross[half:, half:])
    for piece in (1, 2, 3):
        pieces[piece, half:] = jnp.zeros((EXTRA, half), F32)
    for offset, out in enumerate(outs):
        out[...] = pieces[corner ^ offset]


def sum_kernel(*refs):
    ins, out = refs[:-1], refs[-1]
    total = ins[0][...]
    for ref in ins[1:]:
        total = total + ref[...]
    out[...] = total


def symmetric(block, extra):
    half = block.shape[0]
    row = lax.broadcasted_iota(jnp.int32, (half, half), 0)
    col = lax.broadcasted_iota(jnp.int32, (half, half), 1)
    turned = block.T
    first = jnp.where(col >= row, block, turned)
    second = jnp.where(col > row, turned, jnp.where(col < row, block, extra[:1]))
    return first, second


def beside(left, right):
    return jnp.concatenate([left, right], axis=1)


def above(top, bottom):
    return jnp.concatenate([top, bottom], axis=0)


def skew_of(gram):
    width = gram.shape[0]
    row = lax.broadcasted_iota(jnp.int32, (width, width), 0)
    col = lax.broadcasted_iota(jnp.int32, (width, width), 1)
    on_diagonal = row == col
    diagonal = jnp.where(on_diagonal, gram, 0.0)
    inverse_row = 1.0 / jnp.sqrt(jnp.sum(diagonal, axis=0, keepdims=True) + 1e-06)
    inverse_col = 1.0 / jnp.sqrt(jnp.sum(diagonal, axis=1, keepdims=True) + 1e-06)
    scaled = gram * inverse_col * inverse_row
    raw = jnp.where(on_diagonal, 0.0, jnp.where(col > row, scaled, -scaled))
    bound = jnp.max(jnp.sum(jnp.abs(raw), axis=0, keepdims=True), axis=1, keepdims=True)
    return raw * (1.0 / (1.0 + 2.0 * bound))


def each(function, *lists):
    return [function(*entries) for entries in zip(*lists, strict=True)]


def cayleys_of(grams):
    width = grams[0].shape[0]
    row = lax.broadcasted_iota(jnp.int32, (width, width), 0)
    col = lax.broadcasted_iota(jnp.int32, (width, width), 1)
    identity = jnp.where(row == col, 1.0, 0.0)
    skew = each(skew_of, grams)
    skew_parts = each(split, skew)
    square = each(dot3, skew_parts, skew_parts)
    square_parts = each(split, square)
    fourth = each(dot3, square_parts, square_parts)
    cube = each(dot3, skew_parts, square_parts)
    fourth_parts = each(split, fourth)
    eighth = each(lambda parts: dot(parts[0], parts[0]), fourth_parts)
    base = each(lambda s, y, c, f: identity + 2.0 * (s + y + c) + f, skew, square, cube, fourth)
    base = each(lambda b, parts: b + dot3(split(b), parts), base, fourth_parts)
    return each(lambda b, e: b + dot(b.astype(BF16), e.astype(BF16)), base, eighth)


def whole(blocks):
    return above(beside(*blocks[0]), beside(*blocks[1]))


def quarters(x):
    half = x.shape[0] // 2
    return (x[:half, :half], x[:half, half:]), (x[half:, :half], x[half:, half:])


def rounds_kernel(shifts, *refs):
    mine, theirs, (own_high, own_low, other_high, other_low), out = (
        refs[:4],
        refs[4:8],
        refs[8:12],
        refs[12],
    )
    pieces, high, low, turn_high, turn_low, scalars, arrived = refs[13:]
    fetch = pltpu.make_async_copy(shifts, scalars, arrived)
    fetch.start()
    position = lax.axis_index("pos")
    corner = lax.axis_index("rows") % 4
    width = own_high.shape[1]
    half = width // 2
    for held, place in ((mine, position), (theirs, 1 - position)):
        for offset in range(4):
            pieces[place, corner ^ offset] = held[offset][...]
    for side in range(2):
        cols = slice(side * half, (side + 1) * half)
        high[side, position], low[side, position] = own_high[:, cols], own_low[:, cols]
        high[side, 1 - position], low[side, 1 - position] = other_high[:, cols], other_low[:, cols]
    grams = []
    for place in range(2):
        first, second = symmetric(pieces[place, 0, :half], pieces[place, 0, half:])
        between = pieces[place, 1, :half]
        grams.append([[first, between], [between.T, second]])
    cross = [[pieces[0, 2 + side, :half], pieces[1, 2 + side, :half].T] for side in range(2)]
    fetch.wait()
    for step in range(ROUNDS):
        odd = scalars[step] % 2
        turns = each(split, cayleys_of([whole(blocks) for blocks in grams]))
        if step == ROUNDS - 1:
            for place in range(2):
                turn_high[place], turn_low[place] = turns[place]
            for side, place in ((0, position), (1, (position + odd) % 2)):
                held = tuple(beside(x[0, place], x[1, place]) for x in (high, low))
                cols = slice(side * half, (side + 1) * half)
                turn = turn_high[place, :, cols], turn_low[place, :, cols]
                out[:, cols] = dot3(held, turn)
            break
        full = [whole(blocks) for blocks in grams + [cross]]
        right = each(dot3, each(split, full), [turns[0], turns[1], turns[1]])
        zero, one, between = each(
            lambda turn, parts: dot3(turn, parts, 0),
            [turns[0], turns[1], turns[0]],
            each(split, right),
        )
        pick = functools.partial(jnp.where, odd == 1)
        (z_aa, z_ab), (z_ba, z_bb) = quarters(zero)
        (o_aa, o_ab), (o_ba, o_bb) = quarters(one)
        (c_aa, c_ab), (c_ba, c_bb) = quarters(between)
        grams = [
            [[z_aa, pick(c_ab, z_ab)], [pick(c_ab.T, z_ba), pick(o_bb, z_bb)]],
            [[o_aa, pick(c_ba.T, o_ab)], [pick(c_ba, o_ba), pick(z_bb, o_bb)]],
        ]
        cross = [[c_aa, pick(z_ab, c_ab)], [pick(o_ba, c_ba), pick(c_bb.T, c_bb)]]
        moved = []
        for place in range(2):
            held = tuple(beside(x[0, place], x[1, place]) for x in (high, low))
            moved.append(dot3(held, turns[place]))
        for place in range(2):
            high[0, place], low[0, place] = split(moved[place][:, :half])
            to = (place + odd) % 2
            high[1, to], low[1, to] = split(moved[place][:, half:])


def kernel_of(body, out_shape, ins, scratch=()):
    return pl.pallas_call(
        body,
        out_shape=out_shape,
        in_specs=ins,
        out_specs=jax.tree.map(lambda _: VMEM, out_shape),
        scratch_shapes=list(scratch),
        compiler_params=pltpu.CompilerParams(vmem_limit_bytes=40 * 2**20),
    )


def across(x, mask):
    size = lax.axis_size("rows")
    return lax.ppermute(x, "rows", [(i, i ^ mask) for i in range(size)])


def swapped(x):
    return lax.ppermute(x, "pos", [(0, 1), (1, 0)])


def one_sum(matrix, shifts):
    rows, width = matrix.shape
    half = width // 2
    piece = jax.ShapeDtypeStruct((half + EXTRA, half), F32)
    part = jax.ShapeDtypeStruct((rows, width), BF16)
    square = jax.ShapeDtypeStruct((width, width), F32)
    size = lax.axis_size("rows")
    other = swapped(matrix)
    own_high, own_low, own_gram = kernel_of(
        own_kernel,
        [part, part, square],
        [HBM],
        [pltpu.VMEM(matrix.shape, F32), pltpu.SemaphoreType.DMA((CHUNKS,))],
    )(pltpu.with_memory_space_constraint(matrix, pltpu.HBM))
    *pieces, other_high, other_low = kernel_of(
        gram_kernel,
        [piece] * 4 + [part, part],
        [VMEM] * 4,
        [pltpu.VMEM((4,) + piece.shape, F32)],
    )(other, own_high, own_low, own_gram)

    def total(*arrays):
        return kernel_of(sum_kernel, piece, [VMEM] * len(arrays))(*arrays)

    held = total(pieces[0], *[across(pieces[mask], mask) for mask in (1, 2, 3)])
    held = total(held, *[across(held, mask) for mask in range(4, size, 4)])
    mine = [held] + [across(held, mask) for mask in (1, 2, 3)]
    theirs = [swapped(x) for x in mine]
    return kernel_of(
        rounds_kernel,
        jax.ShapeDtypeStruct((rows, width), F32),
        [HBM] + [VMEM] * 12,
        [
            pltpu.VMEM((2, 4) + piece.shape, F32),
            pltpu.VMEM((2, 2, rows, half), BF16),
            pltpu.VMEM((2, 2, rows, half), BF16),
            pltpu.VMEM((2, width, width), BF16),
            pltpu.VMEM((2, width, width), BF16),
            pltpu.SMEM(shifts.shape, jnp.int32),
            pltpu.SemaphoreType.DMA,
        ],
    )(pltpu.with_memory_space_constraint(shifts, pltpu.HBM), *mine, *theirs, own_high, own_low, other_high, other_low)


def solution(mesh):
    placed = (P("rows", "pos"), P())
    plan = one_sum if mesh.shape["pos"] == 2 and mesh.shape["rows"] == 16 else shards
    return jax.shard_map(
        plan, mesh=mesh, in_specs=placed, out_specs=P("rows", "pos"), check_vma=False
    )
```

time: 43.4 us -> 37.9 us (0.87)
  Pallas kernels: 13.8 us -> 11.1 us
  waiting for transfers between devices: 15.1 us -> 13.5 us
  local copies, waits for them, and re-layouts: 1.05 us -> 0 us
    pallas_call x2 -> x3, Pallas kernels: 13.8 us -> 11.1 us  [the longest x1 8.88 us: one_sum(): kernel_of(rounds_kernel, jax.ShapeDtypeStruct((rows, width), F32), [HBM]...]
    ppermute x5, waiting for transfers between devices: 2.85 us -> 1.26 us  [swapped(): return lax.ppermute(x, 'pos', [(0, 1), (1, 0)])]
    unnamed x6 -> x0, local copies, waits for them, and re-layouts: 1.05 us -> none
  transfers between devices with their start and end apart: 14 -> 14, of which waited for: 12 -> 11; matrix products, arithmetic and copies ran while one was open for 0% -> 0% of each run, Pallas kernels for 0% -> 5%
where the time goes in v2:
time: 37.9 us; the launch traced here: 37.8 us
  waiting for transfers between devices  13.5 us (36%)
  starting transfers between devices  13.1 us (35%)
  Pallas kernels  11.1 us (29%)
    ppermute x9, starting transfers between devices, across(): return lax.ppermute(x, 'rows', [(i, i ^ mask) for i in range(size)])  12.4 us
    ppermute x9, waiting for transfers between devices, across(): return lax.ppermute(x, 'rows', [(i, i ^ mask) for i in range(size)])  12.3 us
    pallas_call x1, Pallas kernels, one_sum(): kernel_of(rounds_kernel, jax.ShapeDtypeStruct((rows, width), F32), [HBM]...  8.88 us
    pallas_call x1, Pallas kernels, one_sum(): kernel_of(own_kernel, [part, part, square], [HBM], [pltpu.VMEM(matrix.sha...  1.75 us
    ppermute x5, waiting for transfers between devices, swapped(): return lax.ppermute(x, 'pos', [(0, 1), (1, 0)])  1.26 us
  transfers between devices with their start and end apart: 14, of which 11 were waited for; matrix products, arithmetic and copies ran while one was open for 0% of the time, Pallas kernels for 5%

profile of v2, /device:TPU:0, one launch (start us, length us, event | category | flops | bytes accessed | tf_op | source)
XLA Modules:
  0.0 37.8 jit_solution(1607692400362275439)
XLA Ops:
  0.0 0.5 %collective-permute-start = (f32[512,256]{1,0:T(8,128)}, f32[512,256]{1,0:T(8,128)S(1)}, u32[]{:S(2)}, u32[]{:S(2)}) collective-permute-start(f32[512,256]{1,0:T(8,128)} %own.1), channel_id=1, source_target_pairs={{0,16},{16,0},{1,17},{17,1},{2,18},{18,2},{3,19},{19,3},{4,20},{20... | collective-permute-start | bytes 1572872 | tf_op jit(solution)/shard_map/ppermute | solution.py:293
  0.5 1.8 %shard_map.28 = (bf16[512,256]{1,0:T(8,128)(2,1)S(1)}, bf16[512,256]{1,0:T(8,128)(2,1)S(1)}, f32[256,256]{1,0:T(8,128)S(1)}) custom-call(f32[512,256]{1,0:T(8,128)} %own.1), custom_call_target="tpu_custom_call" | custom-call | tf_op jit(solution)/shard_map/pallas_call | solution.py:304
  2.2 0.0 collective-permute-done.other
  2.2 0.4 %shard_map.29 = (f32[136,128]{1,0:T(8,128)S(1)}, f32[136,128]{1,0:T(8,128)S(1)}, f32[136,128]{1,0:T(8,128)S(1)}, f32[136,128]{1,0:T(8,128)S(1)}, bf16[512,256]{1...) custom-call(f32[512,256]{1,0:T(8,128)S(1)} %collective-permute-done.other, ...), custom_call_target="tpu_custom_call" | custom-call | tf_op jit(solution)/shard_map/pallas_call | solution.py:310
  2.7 2.9 %collective-permute-start.1 = (f32[136,128]{1,0:T(8,128)S(1)}, f32[136,128]{1,0:T(8,128)S(1)}, u32[]{:S(2)}, u32[]{:S(2)}) collective-permute-start(f32[136,128]{1,0:T(8,128)S(1)} %get-tuple-element.18), channel_id=1, source_target_pairs={{0,1},{1,0},{2,3},{3,2},{4,5},{5,4},{6,7},{7,6},{8,9},{9,8},{10,11... | collective-permute-start | bytes 208904 | tf_op jit(solution)/shard_map/ppermute | solution.py:289
  5.6 1.5 %collective-permute-start.2 = (f32[136,128]{1,0:T(8,128)S(1)}, f32[136,128]{1,0:T(8,128)S(1)}, u32[]{:S(2)}, u32[]{:S(2)}) collective-permute-start(f32[136,128]{1,0:T(8,128)S(1)} %get-tuple-element.19), channel_id=1, source_target_pairs={{0,2},{1,3},{2,0},{3,1},{4,6},{5,7},{6,4},{7,5},{8,10},{9,11},{10,... | collective-permute-start | bytes 208904 | tf_op jit(solution)/shard_map/ppermute | solution.py:289
  7.1 0.0 collective-permute-start.3
  7.1 1.0 %collective-permute-done.1.refs_1_ = f32[136,128]{1,0:T(8,128)S(1)} collective-permute-done((f32[136,128]{1,0:T(8,128)S(1)}, f32[136,128]{1,0:T(8,128)S(1)}, u32[]{:S(2)}, u32[]{:S(2)}) %collective-permute-start.1) | collective-permute-done | bytes 69664 | tf_op jit(solution)/shard_map/ppermute | solution.py:289
  8.1 1.8 %collective-permute-done.2.refs_2_ = f32[136,128]{1,0:T(8,128)S(1)} collective-permute-done((f32[136,128]{1,0:T(8,128)S(1)}, f32[136,128]{1,0:T(8,128)S(1)}, u32[]{:S(2)}, u32[]{:S(2)}) %collective-permute-start.2) | collective-permute-done | bytes 69664 | tf_op jit(solution)/shard_map/ppermute | solution.py:289
  9.9 2.4 %collective-permute-done.3.refs_3_ = f32[136,128]{1,0:T(8,128)S(1)} collective-permute-done((f32[136,128]{1,0:T(8,128)S(1)}, f32[136,128]{1,0:T(8,128)S(1)}, u32[]{:S(2)}, u32[]{:S(2)}) %collective-permute-start.3) | collective-permute-done | bytes 69664 | tf_op jit(solution)/shard_map/ppermute | solution.py:289
  12.3 3.7 %collective-permute-start.6 = (f32[136,128]{1,0:T(8,128)S(1)}, f32[136,128]{1,0:T(8,128)S(1)}, u32[]{:S(2)}, u32[]{:S(2)}) collective-permute-start(f32[136,128]{1,0:T(8,128)S(1)} %shard_map.30.refs_0_), channel_id=1, source_target_pairs={{0,12},{1,13},{2,14},{3,15},{4,8},{5,9},{6,10},{7,11},{8,4},{9,5},... | collective-permute-start | bytes 208904 | tf_op jit(solution)/shard_map/ppermute | solution.py:289
  16.0 0.0 collective-permute-start.5
  16.0 0.8 %collective-permute-start.4 = (f32[136,128]{1,0:T(8,128)S(1)}, f32[136,128]{1,0:T(8,128)S(1)}, u32[]{:S(2)}, u32[]{:S(2)}) collective-permute-start(f32[136,128]{1,0:T(8,128)S(1)} %shard_map.30.refs_0_), channel_id=1, source_target_pairs={{0,4},{1,5},{2,6},{3,7},{4,0},{5,1},{6,2},{7,3},{8,12},{9,13},{10,... | collective-permute-start | bytes 208904 | tf_op jit(solution)/shard_map/ppermute | solution.py:289
  16.8 1.7 %collective-permute-done.6.refs_3_ = f32[136,128]{1,0:T(8,128)S(1)} collective-permute-done((f32[136,128]{1,0:T(8,128)S(1)}, f32[136,128]{1,0:T(8,128)S(1)}, u32[]{:S(2)}, u32[]{:S(2)}) %collective-permute-start.6) | collective-permute-done | bytes 69664 | tf_op jit(solution)/shard_map/ppermute | solution.py:289
  18.5 2.7 %collective-permute-done.5.refs_2_ = f32[136,128]{1,0:T(8,128)S(1)} collective-permute-done((f32[136,128]{1,0:T(8,128)S(1)}, f32[136,128]{1,0:T(8,128)S(1)}, u32[]{:S(2)}, u32[]{:S(2)}) %collective-permute-start.5) | collective-permute-done | bytes 69664 | tf_op jit(solution)/shard_map/ppermute | solution.py:289
  21.2 0.0 collective-permute-done.4.refs_1_
  21.2 0.6 %collective-permute-start.9 = (f32[136,128]{1,0:T(8,128)S(1)}, f32[136,128]{1,0:T(8,128)S(1)}, u32[]{:S(2)}, u32[]{:S(2)}) collective-permute-start(f32[136,128]{1,0:T(8,128)S(1)} %shard_map.31.refs_0_), channel_id=1, source_target_pairs={{0,3},{1,2},{2,1},{3,0},{4,7},{5,6},{6,5},{7,4},{8,11},{9,10},{10,... | collective-permute-start | bytes 208904 | tf_op jit(solution)/shard_map/ppermute | solution.py:289
  21.9 1.5 %collective-permute-start.8 = (f32[136,128]{1,0:T(8,128)S(1)}, f32[136,128]{1,0:T(8,128)S(1)}, u32[]{:S(2)}, u32[]{:S(2)}) collective-permute-start(f32[136,128]{1,0:T(8,128)S(1)} %shard_map.31.refs_0_), channel_id=1, source_target_pairs={{0,2},{1,3},{2,0},{3,1},{4,6},{5,7},{6,4},{7,5},{8,10},{9,11},{10,... | collective-permute-start | bytes 208904 | tf_op jit(solution)/shard_map/ppermute | solution.py:289
  23.3 1.4 %collective-permute-start.7 = (f32[136,128]{1,0:T(8,128)S(1)}, f32[136,128]{1,0:T(8,128)S(1)}, u32[]{:S(2)}, u32[]{:S(2)}) collective-permute-start(f32[136,128]{1,0:T(8,128)S(1)} %shard_map.31.refs_0_), channel_id=1, source_target_pairs={{0,1},{1,0},{2,3},{3,2},{4,5},{5,4},{6,7},{7,6},{8,9},{9,8},{10,11... | collective-permute-start | bytes 208904 | tf_op jit(solution)/shard_map/ppermute | solution.py:289
  24.8 0.0 collective-permute-start.10
  24.8 1.8 %collective-permute-done.9.refs_3_ = f32[136,128]{1,0:T(8,128)S(1)} collective-permute-done((f32[136,128]{1,0:T(8,128)S(1)}, f32[136,128]{1,0:T(8,128)S(1)}, u32[]{:S(2)}, u32[]{:S(2)}) %collective-permute-start.9) | collective-permute-done | bytes 69664 | tf_op jit(solution)/shard_map/ppermute | solution.py:289
  26.6 0.0 collective-permute-start.13
  26.6 0.3 collective-permute-done.8.refs_2_
  26.9 0.2 collective-permute-start.12
  27.1 0.5 %collective-permute-done.7.refs_1_ = f32[136,128]{1,0:T(8,128)S(1)} collective-permute-done((f32[136,128]{1,0:T(8,128)S(1)}, f32[136,128]{1,0:T(8,128)S(1)}, u32[]{:S(2)}, u32[]{:S(2)}) %collective-permute-start.7) | collective-permute-done | bytes 69664 | tf_op jit(solution)/shard_map/ppermute | solution.py:289
  27.7 0.0 collective-permute-start.11
  27.7 0.0 collective-permute-done.10.refs_4_
  27.7 0.2 collective-permute-done.13.refs_7_
  27.9 0.3 collective-permute-done.12.refs_6_
  28.2 0.7 %collective-permute-done.11.refs_5_ = f32[136,128]{1,0:T(8,128)S(1)} collective-permute-done((f32[136,128]{1,0:T(8,128)S(1)}, f32[136,128]{1,0:T(8,128)S(1)}, u32[]{:S(2)}, u32[]{:S(2)}) %collective-permute-start.11) | collective-permute-done | bytes 69664 | tf_op jit(solution)/shard_map/ppermute | solution.py:293
  28.9 8.9 %shard_map.32 = f32[512,256]{1,0:T(8,128)} custom-call(s32[3]{0:T(128)} %shifts.1, f32[136,128]{1,0:T(8,128)S(1)} %shard_map.31.refs_0_, f32[136,128]{1,0:T(8,128)S(1)} %collective-permute-done.7.refs_1_, f32[136,128]{1,0:T(8,128)S(1)} %collective-permute-done.8.refs_2_, f32[136,128]{1,0:T(8,128)S(1)} %collective-permute-done.9.refs_3_, ...), custom_call_target="tpu_custom_call" | custom-call | tf_op jit(solution)/shard_map/pallas_call | solution.py:324
  (2 shorter events, 0.1 us)
Async XLA Ops:
  0.0 2.2 %collective-permute-start = (f32[512,256]{1,0:T(8,128)}, f32[512,256]{1,0:T(8,128)S(1)}, u32[]{:S(2)}, u32[]{:S(2)}) collective-permute-start(f32[512,256]{1,0:T(8,128)} %own.1), channel_id=1, source_target_pairs={{0,16},{16,0},{1,17},{17,1},{2,18},{18,2},{3,19},{19,3},{4,20},{20... | collective-permute-start | bytes 1572872 | tf_op jit(solution)/shard_map/ppermute | solution.py:293
  2.7 5.4 %collective-permute-start.1 = (f32[136,128]{1,0:T(8,128)S(1)}, f32[136,128]{1,0:T(8,128)S(1)}, u32[]{:S(2)}, u32[]{:S(2)}) collective-permute-start(f32[136,128]{1,0:T(8,128)S(1)} %get-tuple-element.18), channel_id=1, source_target_pairs={{0,1},{1,0},{2,3},{3,2},{4,5},{5,4},{6,7},{7,6},{8,9},{9,8},{10,11... | collective-permute-start | bytes 208904 | tf_op jit(solution)/shard_map/ppermute | solution.py:289
  5.6 4.3 %collective-permute-start.2 = (f32[136,128]{1,0:T(8,128)S(1)}, f32[136,128]{1,0:T(8,128)S(1)}, u32[]{:S(2)}, u32[]{:S(2)}) collective-permute-start(f32[136,128]{1,0:T(8,128)S(1)} %get-tuple-element.19), channel_id=1, source_target_pairs={{0,2},{1,3},{2,0},{3,1},{4,6},{5,7},{6,4},{7,5},{8,10},{9,11},{10,... | collective-permute-start | bytes 208904 | tf_op jit(solution)/shard_map/ppermute | solution.py:289
  7.1 5.2 %collective-permute-start.3 = (f32[136,128]{1,0:T(8,128)S(1)}, f32[136,128]{1,0:T(8,128)S(1)}, u32[]{:S(2)}, u32[]{:S(2)}) collective-permute-start(f32[136,128]{1,0:T(8,128)S(1)} %get-tuple-element.20), channel_id=1, source_target_pairs={{0,3},{1,2},{2,1},{3,0},{4,7},{5,6},{6,5},{7,4},{8,11},{9,10},{10,... | collective-permute-start | bytes 208904 | tf_op jit(solution)/shard_map/ppermute | solution.py:289
  12.3 6.2 %collective-permute-start.6 = (f32[136,128]{1,0:T(8,128)S(1)}, f32[136,128]{1,0:T(8,128)S(1)}, u32[]{:S(2)}, u32[]{:S(2)}) collective-permute-start(f32[136,128]{1,0:T(8,128)S(1)} %shard_map.30.refs_0_), channel_id=1, source_target_pairs={{0,12},{1,13},{2,14},{3,15},{4,8},{5,9},{6,10},{7,11},{8,4},{9,5},... | collective-permute-start | bytes 208904 | tf_op jit(solution)/shard_map/ppermute | solution.py:289
  16.0 5.2 %collective-permute-start.5 = (f32[136,128]{1,0:T(8,128)S(1)}, f32[136,128]{1,0:T(8,128)S(1)}, u32[]{:S(2)}, u32[]{:S(2)}) collective-permute-start(f32[136,128]{1,0:T(8,128)S(1)} %shard_map.30.refs_0_), channel_id=1, source_target_pairs={{0,8},{1,9},{2,10},{3,11},{4,12},{5,13},{6,14},{7,15},{8,0},{9,1},... | collective-permute-start | bytes 208904 | tf_op jit(solution)/shard_map/ppermute | solution.py:289
  16.0 5.2 %collective-permute-start.4 = (f32[136,128]{1,0:T(8,128)S(1)}, f32[136,128]{1,0:T(8,128)S(1)}, u32[]{:S(2)}, u32[]{:S(2)}) collective-permute-start(f32[136,128]{1,0:T(8,128)S(1)} %shard_map.30.refs_0_), channel_id=1, source_target_pairs={{0,4},{1,5},{2,6},{3,7},{4,0},{5,1},{6,2},{7,3},{8,12},{9,13},{10,... | collective-permute-start | bytes 208904 | tf_op jit(solution)/shard_map/ppermute | solution.py:289
  21.2 5.4 %collective-permute-start.9 = (f32[136,128]{1,0:T(8,128)S(1)}, f32[136,128]{1,0:T(8,128)S(1)}, u32[]{:S(2)}, u32[]{:S(2)}) collective-permute-start(f32[136,128]{1,0:T(8,128)S(1)} %shard_map.31.refs_0_), channel_id=1, source_target_pairs={{0,3},{1,2},{2,1},{3,0},{4,7},{5,6},{6,5},{7,4},{8,11},{9,10},{10,... | collective-permute-start | bytes 208904 | tf_op jit(solution)/shard_map/ppermute | solution.py:289
  21.9 5.1 %collective-permute-start.8 = (f32[136,128]{1,0:T(8,128)S(1)}, f32[136,128]{1,0:T(8,128)S(1)}, u32[]{:S(2)}, u32[]{:S(2)}) collective-permute-start(f32[136,128]{1,0:T(8,128)S(1)} %shard_map.31.refs_0_), channel_id=1, source_target_pairs={{0,2},{1,3},{2,0},{3,1},{4,6},{5,7},{6,4},{7,5},{8,10},{9,11},{10,... | collective-permute-start | bytes 208904 | tf_op jit(solution)/shard_map/ppermute | solution.py:289
  23.3 4.3 %collective-permute-start.7 = (f32[136,128]{1,0:T(8,128)S(1)}, f32[136,128]{1,0:T(8,128)S(1)}, u32[]{:S(2)}, u32[]{:S(2)}) collective-permute-start(f32[136,128]{1,0:T(8,128)S(1)} %shard_map.31.refs_0_), channel_id=1, source_target_pairs={{0,1},{1,0},{2,3},{3,2},{4,5},{5,4},{6,7},{7,6},{8,9},{9,8},{10,11... | collective-permute-start | bytes 208904 | tf_op jit(solution)/shard_map/ppermute | solution.py:289
  24.8 2.9 %collective-permute-start.10 = (f32[136,128]{1,0:T(8,128)S(1)}, f32[136,128]{1,0:T(8,128)S(1)}, u32[]{:S(2)}, u32[]{:S(2)}) collective-permute-start(f32[136,128]{1,0:T(8,128)S(1)} %shard_map.31.refs_0_), channel_id=1, source_target_pairs={{0,16},{16,0},{1,17},{17,1},{2,18},{18,2},{3,19},{19,3},{4,20},{20... | collective-permute-start | bytes 208904 | tf_op jit(solution)/shard_map/ppermute | solution.py:293
  26.6 1.3 %collective-permute-start.13 = (f32[136,128]{1,0:T(8,128)S(1)}, f32[136,128]{1,0:T(8,128)S(1)}, u32[]{:S(2)}, u32[]{:S(2)}) collective-permute-start(f32[136,128]{1,0:T(8,128)S(1)} %collective-permute-done.9.refs_3_), channel_id=1, source_target_pairs={{0,16},{16,0},{1,17},{17,1},{2,18},{18,2},{3,19},{19,3},{4,20},{20... | collective-permute-start | bytes 208904 | tf_op jit(solution)/shard_map/ppermute | solution.py:293
  26.9 1.3 %collective-permute-start.12 = (f32[136,128]{1,0:T(8,128)S(1)}, f32[136,128]{1,0:T(8,128)S(1)}, u32[]{:S(2)}, u32[]{:S(2)}) collective-permute-start(f32[136,128]{1,0:T(8,128)S(1)} %collective-permute-done.8.refs_2_), channel_id=1, source_target_pairs={{0,16},{16,0},{1,17},{17,1},{2,18},{18,2},{3,19},{19,3},{4,20},{20... | collective-permute-start | bytes 208904 | tf_op jit(solution)/shard_map/ppermute | solution.py:293
  27.7 1.3 %collective-permute-start.11 = (f32[136,128]{1,0:T(8,128)S(1)}, f32[136,128]{1,0:T(8,128)S(1)}, u32[]{:S(2)}, u32[]{:S(2)}) collective-permute-start(f32[136,128]{1,0:T(8,128)S(1)} %collective-permute-done.7.refs_1_), channel_id=1, source_target_pairs={{0,16},{16,0},{1,17},{17,1},{2,18},{18,2},{3,19},{19,3},{4,20},{20... | collective-permute-start | bytes 208904 | tf_op jit(solution)/shard_map/ppermute | solution.py:293

commit v3 on v2

--- a/solution.py
+++ b/solution.py
@@ -81,10 +81,10 @@
 
 def dot3(left, right, contract=1):
     (left_high, left_low), (right_high, right_low) = left, right
-    return (
-        dot(left_high, right_low, contract)
-        + dot(left_low, right_high, contract)
-        + dot(left_high, right_high, contract)
+    return dot(
+        jnp.concatenate([left_high, left_low, left_high], axis=contract),
+        jnp.concatenate([right_low, right_high, right_high], axis=0),
+        contract,
     )
 
 
@@ -162,16 +162,24 @@
     return jnp.concatenate([top, bottom], axis=0)
 
 
-def skew_of(gram):
-    width = gram.shape[0]
-    row = lax.broadcasted_iota(jnp.int32, (width, width), 0)
-    col = lax.broadcasted_iota(jnp.int32, (width, width), 1)
-    on_diagonal = row == col
-    diagonal = jnp.where(on_diagonal, gram, 0.0)
-    inverse_row = 1.0 / jnp.sqrt(jnp.sum(diagonal, axis=0, keepdims=True) + 1e-06)
-    inverse_col = 1.0 / jnp.sqrt(jnp.sum(diagonal, axis=1, keepdims=True) + 1e-06)
-    scaled = gram * inverse_col * inverse_row
-    raw = jnp.where(on_diagonal, 0.0, jnp.where(col > row, scaled, -scaled))
+def inverse_norms(block, on_diagonal):
+    diagonal = jnp.where(on_diagonal, block, 0.0)
+    return tuple(
+        1.0 / jnp.sqrt(jnp.sum(diagonal, axis=axis, keepdims=True) + 1e-06) for axis in (1, 0)
+    )
+
+
+def skew_of(blocks):
+    (aa, ab), (ba, bb) = blocks
+    half = aa.shape[0]
+    row = lax.broadcasted_iota(jnp.int32, (half, half), 0)
+    col = lax.broadcasted_iota(jnp.int32, (half, half), 1)
+    side = jnp.where(col > row, 1.0, jnp.where(col < row, -1.0, 0.0))
+    (a_col, a_row), (b_col, b_row) = (inverse_norms(x, col == row) for x in (aa, bb))
+    raw = above(
+        beside(aa * a_col * a_row * side, ab * a_col * b_row),
+        beside(ba * -b_col * a_row, bb * b_col * b_row * side),
+    )
     bound = jnp.max(jnp.sum(jnp.abs(raw), axis=0, keepdims=True), axis=1, keepdims=True)
     return raw * (1.0 / (1.0 + 2.0 * bound))
 
@@ -181,7 +189,7 @@
 
 
 def cayleys_of(grams):
-    width = grams[0].shape[0]
+    width = 2 * grams[0][0][0].shape[0]
     row = lax.broadcasted_iota(jnp.int32, (width, width), 0)
     col = lax.broadcasted_iota(jnp.int32, (width, width), 1)
     identity = jnp.where(row == col, 1.0, 0.0)
@@ -194,8 +202,15 @@
     fourth_parts = each(split, fourth)
     eighth = each(lambda parts: dot(parts[0], parts[0]), fourth_parts)
     base = each(lambda s, y, c, f: identity + 2.0 * (s + y + c) + f, skew, square, cube, fourth)
-    base = each(lambda b, parts: b + dot3(split(b), parts), base, fourth_parts)
-    return each(lambda b, e: b + dot(b.astype(BF16), e.astype(BF16)), base, eighth)
+    base = each(
+        lambda b, f, parts: b + f + dot((b - identity).astype(BF16), parts[0]),
+        base,
+        fourth,
+        fourth_parts,
+    )
+    return each(
+        lambda b, e: b + e + dot((b - identity).astype(BF16), e.astype(BF16)), base, eighth
+    )
 
 
 def whole(blocks):
@@ -234,11 +249,10 @@
         between = pieces[place, 1, :half]
         grams.append([[first, between], [between.T, second]])
     cross = [[pieces[0, 2 + side, :half], pieces[1, 2 + side, :half].T] for side in range(2)]
-    fetch.wait()
     for step in range(ROUNDS):
-        odd = scalars[step] % 2
-        turns = each(split, cayleys_of([whole(blocks) for blocks in grams]))
+        turns = each(split, cayleys_of(grams))
         if step == ROUNDS - 1:
+            odd = scalars[step] % 2
             for place in range(2):
                 turn_high[place], turn_low[place] = turns[place]
             for side, place in ((0, position), (1, (position + odd) % 2)):
@@ -254,6 +268,9 @@
             [turns[0], turns[1], turns[0]],
             each(split, right),
         )
+        if step == 0:
+            fetch.wait()
+        odd = scalars[step] % 2
         pick = functools.partial(jnp.where, odd == 1)
         (z_aa, z_ab), (z_ba, z_bb) = quarters(zero)
         (o_aa, o_ab), (o_ba, o_bb) = quarters(one)

time: 37.9 us -> 37.1 us (0.979)
  Pallas kernels: 11.1 us -> 9.98 us
    pallas_call x1, Pallas kernels: 8.88 us -> 8.03 us  [one_sum(): kernel_of(rounds_kernel, jax.ShapeDtypeStruct((rows, width), F32), [HBM]...]
  transfers between devices with their start and end apart: 14 -> 14, of which waited for: 11 -> 12; matrix products, arithmetic and copies ran while one was open for 0% -> 0% of each run, Pallas kernels for 5% -> 4%
where the time goes in v3:
time: 37.1 us; the launch traced here: 36.9 us
  waiting for transfers between devices  13.8 us (37%)
  starting transfers between devices  13.1 us (35%)
  Pallas kernels  9.98 us (27%)
    ppermute x9, starting transfers between devices, across(): return lax.ppermute(x, 'rows', [(i, i ^ mask) for i in range(size)])  12.5 us
    ppermute x9, waiting for transfers between devices, across(): return lax.ppermute(x, 'rows', [(i, i ^ mask) for i in range(size)])  12.3 us
    pallas_call x1, Pallas kernels, one_sum(): kernel_of(rounds_kernel, jax.ShapeDtypeStruct((rows, width), F32), [HBM]...  8.03 us
    ppermute x5, waiting for transfers between devices, swapped(): return lax.ppermute(x, 'pos', [(0, 1), (1, 0)])  1.53 us
    pallas_call x1, Pallas kernels, one_sum(): kernel_of(own_kernel, [part, part, square], [HBM], [pltpu.VMEM(matrix.sha...  1.46 us
  transfers between devices with their start and end apart: 14, of which 12 were waited for; matrix products, arithmetic and copies ran while one was open for 0% of the time, Pallas kernels for 4%

profile of v3, /device:TPU:0, one launch (start us, length us, event | category | flops | bytes accessed | tf_op | source)
XLA Modules:
  0.0 36.9 jit_solution(5491439098593450523)
XLA Ops:
  0.0 0.5 %collective-permute-start = (f32[512,256]{1,0:T(8,128)}, f32[512,256]{1,0:T(8,128)S(1)}, u32[]{:S(2)}, u32[]{:S(2)}) collective-permute-start(f32[512,256]{1,0:T(8,128)} %own.1), channel_id=1, source_target_pairs={{0,16},{16,0},{1,17},{17,1},{2,18},{18,2},{3,19},{19,3},{4,20},{20... | collective-permute-start | bytes 1572872 | tf_op jit(solution)/shard_map/ppermute | solution.py:310
  0.5 1.5 %shard_map.28 = (bf16[512,256]{1,0:T(8,128)(2,1)S(1)}, bf16[512,256]{1,0:T(8,128)(2,1)S(1)}, f32[256,256]{1,0:T(8,128)S(1)}) custom-call(f32[512,256]{1,0:T(8,128)} %own.1), custom_call_target="tpu_custom_call" | custom-call | tf_op jit(solution)/shard_map/pallas_call | solution.py:321
  1.9 0.3 collective-permute-done.other
  2.2 0.4 %shard_map.29 = (f32[136,128]{1,0:T(8,128)S(1)}, f32[136,128]{1,0:T(8,128)S(1)}, f32[136,128]{1,0:T(8,128)S(1)}, f32[136,128]{1,0:T(8,128)S(1)}, bf16[512,256]{1...) custom-call(f32[512,256]{1,0:T(8,128)S(1)} %collective-permute-done.other, ...), custom_call_target="tpu_custom_call" | custom-call | tf_op jit(solution)/shard_map/pallas_call | solution.py:327
  2.6 2.9 %collective-permute-start.1 = (f32[136,128]{1,0:T(8,128)S(1)}, f32[136,128]{1,0:T(8,128)S(1)}, u32[]{:S(2)}, u32[]{:S(2)}) collective-permute-start(f32[136,128]{1,0:T(8,128)S(1)} %get-tuple-element.18), channel_id=1, source_target_pairs={{0,1},{1,0},{2,3},{3,2},{4,5},{5,4},{6,7},{7,6},{8,9},{9,8},{10,11... | collective-permute-start | bytes 208904 | tf_op jit(solution)/shard_map/ppermute | solution.py:306
  5.6 1.5 %collective-permute-start.2 = (f32[136,128]{1,0:T(8,128)S(1)}, f32[136,128]{1,0:T(8,128)S(1)}, u32[]{:S(2)}, u32[]{:S(2)}) collective-permute-start(f32[136,128]{1,0:T(8,128)S(1)} %get-tuple-element.19), channel_id=1, source_target_pairs={{0,2},{1,3},{2,0},{3,1},{4,6},{5,7},{6,4},{7,5},{8,10},{9,11},{10,... | collective-permute-start | bytes 208904 | tf_op jit(solution)/shard_map/ppermute | solution.py:306
  7.1 0.0 collective-permute-start.3
  7.1 0.9 %collective-permute-done.1.refs_1_ = f32[136,128]{1,0:T(8,128)S(1)} collective-permute-done((f32[136,128]{1,0:T(8,128)S(1)}, f32[136,128]{1,0:T(8,128)S(1)}, u32[]{:S(2)}, u32[]{:S(2)}) %collective-permute-start.1) | collective-permute-done | bytes 69664 | tf_op jit(solution)/shard_map/ppermute | solution.py:306
  8.0 1.8 %collective-permute-done.2.refs_2_ = f32[136,128]{1,0:T(8,128)S(1)} collective-permute-done((f32[136,128]{1,0:T(8,128)S(1)}, f32[136,128]{1,0:T(8,128)S(1)}, u32[]{:S(2)}, u32[]{:S(2)}) %collective-permute-start.2) | collective-permute-done | bytes 69664 | tf_op jit(solution)/shard_map/ppermute | solution.py:306
  9.9 2.4 %collective-permute-done.3.refs_3_ = f32[136,128]{1,0:T(8,128)S(1)} collective-permute-done((f32[136,128]{1,0:T(8,128)S(1)}, f32[136,128]{1,0:T(8,128)S(1)}, u32[]{:S(2)}, u32[]{:S(2)}) %collective-permute-start.3) | collective-permute-done | bytes 69664 | tf_op jit(solution)/shard_map/ppermute | solution.py:306
  12.3 3.7 %collective-permute-start.6 = (f32[136,128]{1,0:T(8,128)S(1)}, f32[136,128]{1,0:T(8,128)S(1)}, u32[]{:S(2)}, u32[]{:S(2)}) collective-permute-start(f32[136,128]{1,0:T(8,128)S(1)} %shard_map.30.refs_0_), channel_id=1, source_target_pairs={{0,12},{1,13},{2,14},{3,15},{4,8},{5,9},{6,10},{7,11},{8,4},{9,5},... | collective-permute-start | bytes 208904 | tf_op jit(solution)/shard_map/ppermute | solution.py:306
  16.0 0.0 collective-permute-start.5
  16.0 0.8 %collective-permute-start.4 = (f32[136,128]{1,0:T(8,128)S(1)}, f32[136,128]{1,0:T(8,128)S(1)}, u32[]{:S(2)}, u32[]{:S(2)}) collective-permute-start(f32[136,128]{1,0:T(8,128)S(1)} %shard_map.30.refs_0_), channel_id=1, source_target_pairs={{0,4},{1,5},{2,6},{3,7},{4,0},{5,1},{6,2},{7,3},{8,12},{9,13},{10,... | collective-permute-start | bytes 208904 | tf_op jit(solution)/shard_map/ppermute | solution.py:306
  16.8 1.7 %collective-permute-done.6.refs_3_ = f32[136,128]{1,0:T(8,128)S(1)} collective-permute-done((f32[136,128]{1,0:T(8,128)S(1)}, f32[136,128]{1,0:T(8,128)S(1)}, u32[]{:S(2)}, u32[]{:S(2)}) %collective-permute-start.6) | collective-permute-done | bytes 69664 | tf_op jit(solution)/shard_map/ppermute | solution.py:306
  18.5 2.7 %collective-permute-done.5.refs_2_ = f32[136,128]{1,0:T(8,128)S(1)} collective-permute-done((f32[136,128]{1,0:T(8,128)S(1)}, f32[136,128]{1,0:T(8,128)S(1)}, u32[]{:S(2)}, u32[]{:S(2)}) %collective-permute-start.5) | collective-permute-done | bytes 69664 | tf_op jit(solution)/shard_map/ppermute | solution.py:306
  21.2 0.0 collective-permute-done.4.refs_1_
  21.2 0.7 %collective-permute-start.9 = (f32[136,128]{1,0:T(8,128)S(1)}, f32[136,128]{1,0:T(8,128)S(1)}, u32[]{:S(2)}, u32[]{:S(2)}) collective-permute-start(f32[136,128]{1,0:T(8,128)S(1)} %shard_map.31.refs_0_), channel_id=1, source_target_pairs={{0,3},{1,2},{2,1},{3,0},{4,7},{5,6},{6,5},{7,4},{8,11},{9,10},{10,... | collective-permute-start | bytes 208904 | tf_op jit(solution)/shard_map/ppermute | solution.py:306
  21.9 1.5 %collective-permute-start.8 = (f32[136,128]{1,0:T(8,128)S(1)}, f32[136,128]{1,0:T(8,128)S(1)}, u32[]{:S(2)}, u32[]{:S(2)}) collective-permute-start(f32[136,128]{1,0:T(8,128)S(1)} %shard_map.31.refs_0_), channel_id=1, source_target_pairs={{0,2},{1,3},{2,0},{3,1},{4,6},{5,7},{6,4},{7,5},{8,10},{9,11},{10,... | collective-permute-start | bytes 208904 | tf_op jit(solution)/shard_map/ppermute | solution.py:306
  23.3 1.4 %collective-permute-start.7 = (f32[136,128]{1,0:T(8,128)S(1)}, f32[136,128]{1,0:T(8,128)S(1)}, u32[]{:S(2)}, u32[]{:S(2)}) collective-permute-start(f32[136,128]{1,0:T(8,128)S(1)} %shard_map.31.refs_0_), channel_id=1, source_target_pairs={{0,1},{1,0},{2,3},{3,2},{4,5},{5,4},{6,7},{7,6},{8,9},{9,8},{10,11... | collective-permute-start | bytes 208904 | tf_op jit(solution)/shard_map/ppermute | solution.py:306
  24.8 0.0 collective-permute-start.10
  24.8 1.8 %collective-permute-done.9.refs_3_ = f32[136,128]{1,0:T(8,128)S(1)} collective-permute-done((f32[136,128]{1,0:T(8,128)S(1)}, f32[136,128]{1,0:T(8,128)S(1)}, u32[]{:S(2)}, u32[]{:S(2)}) %collective-permute-start.9) | collective-permute-done | bytes 69664 | tf_op jit(solution)/shard_map/ppermute | solution.py:306
  26.6 0.0 collective-permute-start.13
  26.6 0.3 collective-permute-done.8.refs_2_
  26.9 0.2 collective-permute-start.12
  27.1 0.5 %collective-permute-done.7.refs_1_ = f32[136,128]{1,0:T(8,128)S(1)} collective-permute-done((f32[136,128]{1,0:T(8,128)S(1)}, f32[136,128]{1,0:T(8,128)S(1)}, u32[]{:S(2)}, u32[]{:S(2)}) %collective-permute-start.7) | collective-permute-done | bytes 69664 | tf_op jit(solution)/shard_map/ppermute | solution.py:306
  27.6 0.0 collective-permute-start.11
  27.7 0.0 collective-permute-done.10.refs_4_
  27.7 0.2 collective-permute-done.13.refs_7_
  27.9 0.3 collective-permute-done.12.refs_6_
  28.2 0.7 %collective-permute-done.11.refs_5_ = f32[136,128]{1,0:T(8,128)S(1)} collective-permute-done((f32[136,128]{1,0:T(8,128)S(1)}, f32[136,128]{1,0:T(8,128)S(1)}, u32[]{:S(2)}, u32[]{:S(2)}) %collective-permute-start.11) | collective-permute-done | bytes 69664 | tf_op jit(solution)/shard_map/ppermute | solution.py:310
  28.9 8.0 %shard_map.32 = f32[512,256]{1,0:T(8,128)} custom-call(s32[3]{0:T(128)} %shifts.1, f32[136,128]{1,0:T(8,128)S(1)} %shard_map.31.refs_0_, f32[136,128]{1,0:T(8,128)S(1)} %collective-permute-done.7.refs_1_, f32[136,128]{1,0:T(8,128)S(1)} %collective-permute-done.8.refs_2_, f32[136,128]{1,0:T(8,128)S(1)} %collective-permute-done.9.refs_3_, ...), custom_call_target="tpu_custom_call" | custom-call | tf_op jit(solution)/shard_map/pallas_call | solution.py:341
  (2 shorter events, 0.1 us)
Async XLA Ops:
  0.0 2.2 %collective-permute-start = (f32[512,256]{1,0:T(8,128)}, f32[512,256]{1,0:T(8,128)S(1)}, u32[]{:S(2)}, u32[]{:S(2)}) collective-permute-start(f32[512,256]{1,0:T(8,128)} %own.1), channel_id=1, source_target_pairs={{0,16},{16,0},{1,17},{17,1},{2,18},{18,2},{3,19},{19,3},{4,20},{20... | collective-permute-start | bytes 1572872 | tf_op jit(solution)/shard_map/ppermute | solution.py:310
  2.6 5.4 %collective-permute-start.1 = (f32[136,128]{1,0:T(8,128)S(1)}, f32[136,128]{1,0:T(8,128)S(1)}, u32[]{:S(2)}, u32[]{:S(2)}) collective-permute-start(f32[136,128]{1,0:T(8,128)S(1)} %get-tuple-element.18), channel_id=1, source_target_pairs={{0,1},{1,0},{2,3},{3,2},{4,5},{5,4},{6,7},{7,6},{8,9},{9,8},{10,11... | collective-permute-start | bytes 208904 | tf_op jit(solution)/shard_map/ppermute | solution.py:306
  5.6 4.3 %collective-permute-start.2 = (f32[136,128]{1,0:T(8,128)S(1)}, f32[136,128]{1,0:T(8,128)S(1)}, u32[]{:S(2)}, u32[]{:S(2)}) collective-permute-start(f32[136,128]{1,0:T(8,128)S(1)} %get-tuple-element.19), channel_id=1, source_target_pairs={{0,2},{1,3},{2,0},{3,1},{4,6},{5,7},{6,4},{7,5},{8,10},{9,11},{10,... | collective-permute-start | bytes 208904 | tf_op jit(solution)/shard_map/ppermute | solution.py:306
  7.1 5.2 %collective-permute-start.3 = (f32[136,128]{1,0:T(8,128)S(1)}, f32[136,128]{1,0:T(8,128)S(1)}, u32[]{:S(2)}, u32[]{:S(2)}) collective-permute-start(f32[136,128]{1,0:T(8,128)S(1)} %get-tuple-element.20), channel_id=1, source_target_pairs={{0,3},{1,2},{2,1},{3,0},{4,7},{5,6},{6,5},{7,4},{8,11},{9,10},{10,... | collective-permute-start | bytes 208904 | tf_op jit(solution)/shard_map/ppermute | solution.py:306
  12.3 6.2 %collective-permute-start.6 = (f32[136,128]{1,0:T(8,128)S(1)}, f32[136,128]{1,0:T(8,128)S(1)}, u32[]{:S(2)}, u32[]{:S(2)}) collective-permute-start(f32[136,128]{1,0:T(8,128)S(1)} %shard_map.30.refs_0_), channel_id=1, source_target_pairs={{0,12},{1,13},{2,14},{3,15},{4,8},{5,9},{6,10},{7,11},{8,4},{9,5},... | collective-permute-start | bytes 208904 | tf_op jit(solution)/shard_map/ppermute | solution.py:306
  16.0 5.2 %collective-permute-start.5 = (f32[136,128]{1,0:T(8,128)S(1)}, f32[136,128]{1,0:T(8,128)S(1)}, u32[]{:S(2)}, u32[]{:S(2)}) collective-permute-start(f32[136,128]{1,0:T(8,128)S(1)} %shard_map.30.refs_0_), channel_id=1, source_target_pairs={{0,8},{1,9},{2,10},{3,11},{4,12},{5,13},{6,14},{7,15},{8,0},{9,1},... | collective-permute-start | bytes 208904 | tf_op jit(solution)/shard_map/ppermute | solution.py:306
  16.0 5.2 %collective-permute-start.4 = (f32[136,128]{1,0:T(8,128)S(1)}, f32[136,128]{1,0:T(8,128)S(1)}, u32[]{:S(2)}, u32[]{:S(2)}) collective-permute-start(f32[136,128]{1,0:T(8,128)S(1)} %shard_map.30.refs_0_), channel_id=1, source_target_pairs={{0,4},{1,5},{2,6},{3,7},{4,0},{5,1},{6,2},{7,3},{8,12},{9,13},{10,... | collective-permute-start | bytes 208904 | tf_op jit(solution)/shard_map/ppermute | solution.py:306
  21.2 5.4 %collective-permute-start.9 = (f32[136,128]{1,0:T(8,128)S(1)}, f32[136,128]{1,0:T(8,128)S(1)}, u32[]{:S(2)}, u32[]{:S(2)}) collective-permute-start(f32[136,128]{1,0:T(8,128)S(1)} %shard_map.31.refs_0_), channel_id=1, source_target_pairs={{0,3},{1,2},{2,1},{3,0},{4,7},{5,6},{6,5},{7,4},{8,11},{9,10},{10,... | collective-permute-start | bytes 208904 | tf_op jit(solution)/shard_map/ppermute | solution.py:306
  21.9 5.1 %collective-permute-start.8 = (f32[136,128]{1,0:T(8,128)S(1)}, f32[136,128]{1,0:T(8,128)S(1)}, u32[]{:S(2)}, u32[]{:S(2)}) collective-permute-start(f32[136,128]{1,0:T(8,128)S(1)} %shard_map.31.refs_0_), channel_id=1, source_target_pairs={{0,2},{1,3},{2,0},{3,1},{4,6},{5,7},{6,4},{7,5},{8,10},{9,11},{10,... | collective-permute-start | bytes 208904 | tf_op jit(solution)/shard_map/ppermute | solution.py:306
  23.3 4.3 %collective-permute-start.7 = (f32[136,128]{1,0:T(8,128)S(1)}, f32[136,128]{1,0:T(8,128)S(1)}, u32[]{:S(2)}, u32[]{:S(2)}) collective-permute-start(f32[136,128]{1,0:T(8,128)S(1)} %shard_map.31.refs_0_), channel_id=1, source_target_pairs={{0,1},{1,0},{2,3},{3,2},{4,5},{5,4},{6,7},{7,6},{8,9},{9,8},{10,11... | collective-permute-start | bytes 208904 | tf_op jit(solution)/shard_map/ppermute | solution.py:306
  24.8 2.9 %collective-permute-start.10 = (f32[136,128]{1,0:T(8,128)S(1)}, f32[136,128]{1,0:T(8,128)S(1)}, u32[]{:S(2)}, u32[]{:S(2)}) collective-permute-start(f32[136,128]{1,0:T(8,128)S(1)} %shard_map.31.refs_0_), channel_id=1, source_target_pairs={{0,16},{16,0},{1,17},{17,1},{2,18},{18,2},{3,19},{19,3},{4,20},{20... | collective-permute-start | bytes 208904 | tf_op jit(solution)/shard_map/ppermute | solution.py:310
  26.6 1.3 %collective-permute-start.13 = (f32[136,128]{1,0:T(8,128)S(1)}, f32[136,128]{1,0:T(8,128)S(1)}, u32[]{:S(2)}, u32[]{:S(2)}) collective-permute-start(f32[136,128]{1,0:T(8,128)S(1)} %collective-permute-done.9.refs_3_), channel_id=1, source_target_pairs={{0,16},{16,0},{1,17},{17,1},{2,18},{18,2},{3,19},{19,3},{4,20},{20... | collective-permute-start | bytes 208904 | tf_op jit(solution)/shard_map/ppermute | solution.py:310
  26.9 1.3 %collective-permute-start.12 = (f32[136,128]{1,0:T(8,128)S(1)}, f32[136,128]{1,0:T(8,128)S(1)}, u32[]{:S(2)}, u32[]{:S(2)}) collective-permute-start(f32[136,128]{1,0:T(8,128)S(1)} %collective-permute-done.8.refs_2_), channel_id=1, source_target_pairs={{0,16},{16,0},{1,17},{17,1},{2,18},{18,2},{3,19},{19,3},{4,20},{20... | collective-permute-start | bytes 208904 | tf_op jit(solution)/shard_map/ppermute | solution.py:310
  27.6 1.3 %collective-permute-start.11 = (f32[136,128]{1,0:T(8,128)S(1)}, f32[136,128]{1,0:T(8,128)S(1)}, u32[]{:S(2)}, u32[]{:S(2)}) collective-permute-start(f32[136,128]{1,0:T(8,128)S(1)} %collective-permute-done.7.refs_1_), channel_id=1, source_target_pairs={{0,16},{16,0},{1,17},{17,1},{2,18},{18,2},{3,19},{19,3},{4,20},{20... | collective-permute-start | bytes 208904 | tf_op jit(solution)/shard_map/ppermute | solution.py:310

commit v4 on v3

--- a/solution.py
+++ b/solution.py
@@ -11,6 +11,12 @@
 NS_STEPS = 3
 EXTRA = 8
 CHUNKS = 2
+PAIRS = {
+    (2, 2): ((0, 1), (1, 0), (0, 0)),
+    (2, 3): ((1, 1), (0, 2), (0, 1), (1, 0), (0, 0)),
+    (3, 2): ((1, 1), (2, 0), (0, 1), (1, 0), (0, 0)),
+    (3, 3): ((1, 1), (0, 2), (2, 0), (0, 1), (1, 0), (0, 0)),
+}
 F32 = jnp.float32
 BF16 = jnp.bfloat16
 VMEM = pl.BlockSpec(memory_space=pltpu.VMEM)
@@ -68,9 +74,13 @@
     return current
 
 
-def split(x):
-    high = x.astype(BF16)
-    return high, (x - high.astype(F32)).astype(BF16)
+def split(x, parts=2):
+    made = []
+    for part in range(parts):
+        made.append(x.astype(BF16))
+        if part < parts - 1:
+            x = x - made[-1].astype(F32)
+    return tuple(made)
 
 
 def dot(left, right, contract=1):
@@ -79,16 +89,16 @@
     )
 
 
-def dot3(left, right, contract=1):
-    (left_high, left_low), (right_high, right_low) = left, right
+def dots(left, right, contract=1):
+    pairs = PAIRS[len(left), len(right)]
     return dot(
-        jnp.concatenate([left_high, left_low, left_high], axis=contract),
-        jnp.concatenate([right_low, right_high, right_high], axis=0),
+        jnp.concatenate([left[a] for a, _ in pairs], axis=contract),
+        jnp.concatenate([right[b] for _, b in pairs], axis=0),
         contract,
     )
 
 
-def own_kernel(own, high, low, gram, landed, arrived):
+def own_kernel(own, high, low, rest, gram, landed, arrived):
     span = own.shape[0] // CHUNKS
     copies = []
     for chunk in range(CHUNKS):
@@ -99,9 +109,9 @@
     for chunk, copy in enumerate(copies):
         rows = slice(chunk * span, (chunk + 1) * span)
         copy.wait()
-        parts = split(landed[rows])
-        high[rows], low[rows] = parts
-        part = dot3(parts, parts, 0)
+        parts = split(landed[rows], 3)
+        high[rows], low[rows], rest[rows] = parts
+        part = dots(parts, parts, 0)
         total = part if total is None else total + part
     gram[...] = total
 
@@ -115,13 +125,14 @@
     return jnp.where(col >= row, first, second), diagonal
 
 
-def gram_kernel(other, own_high, own_low, own_gram, *refs):
+def gram_kernel(other, own_high, own_low, own_rest, own_gram, *refs):
     outs, (high, low, pieces) = refs[:4], refs[4:]
     position = lax.axis_index("pos")
     corner = lax.axis_index("rows") % 4
     half = other.shape[1] // 2
-    high[...], low[...] = split(other[...])
-    cross = dot3((own_high[...], own_low[...]), (high[...], low[...]), 0)
+    parts = split(other[...], 3)
+    high[...], low[...] = parts[:2]
+    cross = dots((own_high[...], own_low[...], own_rest[...]), parts, 0)
     first = position == 0
     gram = own_gram[...]
     square, diagonal = packed(gram)
@@ -165,23 +176,25 @@
 def inverse_norms(block, on_diagonal):
     diagonal = jnp.where(on_diagonal, block, 0.0)
     return tuple(
-        1.0 / jnp.sqrt(jnp.sum(diagonal, axis=axis, keepdims=True) + 1e-06) for axis in (1, 0)
-    )
-
-
-def skew_of(blocks):
+        1.0 / jnp.sqrt(jnp.maximum(jnp.sum(diagonal, axis=axis, keepdims=True), 0.0) + 1e-06)
+        for axis in (1, 0)
+    )
+
+
+def raw_of(blocks):
     (aa, ab), (ba, bb) = blocks
     half = aa.shape[0]
     row = lax.broadcasted_iota(jnp.int32, (half, half), 0)
     col = lax.broadcasted_iota(jnp.int32, (half, half), 1)
     side = jnp.where(col > row, 1.0, jnp.where(col < row, -1.0, 0.0))
     (a_col, a_row), (b_col, b_row) = (inverse_norms(x, col == row) for x in (aa, bb))
+    bounded = functools.partial(jnp.clip, min=-1.0, max=1.0)
     raw = above(
-        beside(aa * a_col * a_row * side, ab * a_col * b_row),
-        beside(ba * -b_col * a_row, bb * b_col * b_row * side),
+        beside(bounded(aa * a_col * a_row) * side, bounded(ab * a_col * b_row)),
+        beside(bounded(ba * -b_col * a_row), bounded(bb * b_col * b_row) * side),
     )
     bound = jnp.max(jnp.sum(jnp.abs(raw), axis=0, keepdims=True), axis=1, keepdims=True)
-    return raw * (1.0 / (1.0 + 2.0 * bound))
+    return raw, 1.0 / (1.0 + 2.0 * bound)
 
 
 def each(function, *lists):
@@ -193,15 +206,22 @@
     row = lax.broadcasted_iota(jnp.int32, (width, width), 0)
     col = lax.broadcasted_iota(jnp.int32, (width, width), 1)
     identity = jnp.where(row == col, 1.0, 0.0)
-    skew = each(skew_of, grams)
-    skew_parts = each(split, skew)
-    square = each(dot3, skew_parts, skew_parts)
+    raw, scale = zip(*each(raw_of, grams), strict=True)
+    raw_parts = each(split, raw)
+    square = each(lambda parts, c: dots(parts, parts) * (c * c), raw_parts, scale)
     square_parts = each(split, square)
-    fourth = each(dot3, square_parts, square_parts)
-    cube = each(dot3, skew_parts, square_parts)
+    fourth = each(dots, square_parts, square_parts)
+    cube = each(dots, raw_parts, square_parts)
     fourth_parts = each(split, fourth)
     eighth = each(lambda parts: dot(parts[0], parts[0]), fourth_parts)
-    base = each(lambda s, y, c, f: identity + 2.0 * (s + y + c) + f, skew, square, cube, fourth)
+    base = each(
+        lambda r, k, y, c, f: identity + 2.0 * ((r + c) * k + y) + f,
+        raw,
+        scale,
+        square,
+        cube,
+        fourth,
+    )
     base = each(
         lambda b, f, parts: b + f + dot((b - identity).astype(BF16), parts[0]),
         base,
@@ -259,14 +279,14 @@
                 held = tuple(beside(x[0, place], x[1, place]) for x in (high, low))
                 cols = slice(side * half, (side + 1) * half)
                 turn = turn_high[place, :, cols], turn_low[place, :, cols]
-                out[:, cols] = dot3(held, turn)
+                out[:, cols] = dots(held, turn)
             break
         full = [whole(blocks) for blocks in grams + [cross]]
-        right = each(dot3, each(split, full), [turns[0], turns[1], turns[1]])
+        right = each(dots, each(functools.partial(split, parts=3), full), [turns[0], turns[1], turns[1]])
         zero, one, between = each(
-            lambda turn, parts: dot3(turn, parts, 0),
+            lambda turn, parts: dots(turn, parts, 0),
             [turns[0], turns[1], turns[0]],
-            each(split, right),
+            each(functools.partial(split, parts=3), right),
         )
         if step == 0:
             fetch.wait()
@@ -283,7 +303,7 @@
         moved = []
         for place in range(2):
             held = tuple(beside(x[0, place], x[1, place]) for x in (high, low))
-            moved.append(dot3(held, turns[place]))
+            moved.append(dots(held, turns[place]))
         for place in range(2):
             high[0, place], low[0, place] = split(moved[place][:, :half])
             to = (place + odd) % 2
@@ -318,18 +338,18 @@
     square = jax.ShapeDtypeStruct((width, width), F32)
     size = lax.axis_size("rows")
     other = swapped(matrix)
-    own_high, own_low, own_gram = kernel_of(
+    own_high, own_low, own_rest, own_gram = kernel_of(
         own_kernel,
-        [part, part, square],
+        [part, part, part, square],
         [HBM],
         [pltpu.VMEM(matrix.shape, F32), pltpu.SemaphoreType.DMA((CHUNKS,))],
     )(pltpu.with_memory_space_constraint(matrix, pltpu.HBM))
     *pieces, other_high, other_low = kernel_of(
         gram_kernel,
         [piece] * 4 + [part, part],
-        [VMEM] * 4,
+        [VMEM] * 5,
         [pltpu.VMEM((4,) + piece.shape, F32)],
-    )(other, own_high, own_low, own_gram)
+    )(other, own_high, own_low, own_rest, own_gram)
 
     def total(*arrays):
         return kernel_of(sum_kernel, piece, [VMEM] * len(arrays))(*arrays)

time: 37.1 us -> 38 us (1.024)
  Pallas kernels: 9.98 us -> 11.1 us
    pallas_call x1, Pallas kernels: 8.03 us -> 8.71 us  [one_sum(): kernel_of(rounds_kernel, jax.ShapeDtypeStruct((rows, width), F32), [HBM]...]
    pallas_call x2, Pallas kernels: 1.89 us -> 2.35 us  [the longest x1 1.68 us: one_sum(): kernel_of(own_kernel, [part, part, part, square], [HBM], [pltpu.VMEM(matr...]
where the time goes in v4:
time: 38 us; the launch traced here: 37.9 us
  waiting for transfers between devices  13.6 us (36%)
  starting transfers between devices  13.1 us (34%)
  Pallas kernels  11.1 us (29%)
    ppermute x9, starting transfers between devices, across(): return lax.ppermute(x, 'rows', [(i, i ^ mask) for i in range(size)])  12.5 us
    ppermute x9, waiting for transfers between devices, across(): return lax.ppermute(x, 'rows', [(i, i ^ mask) for i in range(size)])  12.3 us
    pallas_call x1, Pallas kernels, one_sum(): kernel_of(rounds_kernel, jax.ShapeDtypeStruct((rows, width), F32), [HBM]...  8.71 us
    pallas_call x1, Pallas kernels, one_sum(): kernel_of(own_kernel, [part, part, part, square], [HBM], [pltpu.VMEM(matr...  1.68 us
    ppermute x5, waiting for transfers between devices, swapped(): return lax.ppermute(x, 'pos', [(0, 1), (1, 0)])  1.31 us
  transfers between devices with their start and end apart: 14, of which 12 were waited for; matrix products, arithmetic and copies ran while one was open for 0% of the time, Pallas kernels for 4%

profile of v4, /device:TPU:0, one launch (start us, length us, event | category | flops | bytes accessed | tf_op | source)
XLA Modules:
  0.0 37.9 jit_solution(16465421417008246559)
XLA Ops:
  0.0 0.5 %collective-permute-start = (f32[512,256]{1,0:T(8,128)}, f32[512,256]{1,0:T(8,128)S(1)}, u32[]{:S(2)}, u32[]{:S(2)}) collective-permute-start(f32[512,256]{1,0:T(8,128)} %own.1), channel_id=1, source_target_pairs={{0,16},{16,0},{1,17},{17,1},{2,18},{18,2},{3,19},{19,3},{4,20},{20... | collective-permute-start | bytes 1572872 | tf_op jit(solution)/shard_map/ppermute | solution.py:330
  0.5 1.7 %shard_map.28 = (bf16[512,256]{1,0:T(8,128)(2,1)S(1)}, bf16[512,256]{1,0:T(8,128)(2,1)S(1)}, bf16[512,256]{1,0:T(8,128)(2,1)S(1)}, f32[256,256]{1,0:T(8,128)S(1)}) custom-call(f32[512,256]{1,0:T(8,128)} %own.1), custom_call_target="tpu_custom_call" | custom-call | tf_op jit(solution)/shard_map/pallas_call | solution.py:341
  2.1 0.1 collective-permute-done.other
  2.2 0.7 %shard_map.29 = (f32[136,128]{1,0:T(8,128)S(1)}, f32[136,128]{1,0:T(8,128)S(1)}, f32[136,128]{1,0:T(8,128)S(1)}, f32[136,128]{1,0:T(8,128)S(1)}, bf16[512,256]{1...) custom-call(f32[512,256]{1,0:T(8,128)S(1)} %collective-permute-done.other, ...), custom_call_target="tpu_custom_call" | custom-call | tf_op jit(solution)/shard_map/pallas_call | solution.py:347
  2.9 2.9 %collective-permute-start.1 = (f32[136,128]{1,0:T(8,128)S(1)}, f32[136,128]{1,0:T(8,128)S(1)}, u32[]{:S(2)}, u32[]{:S(2)}) collective-permute-start(f32[136,128]{1,0:T(8,128)S(1)} %get-tuple-element.20), channel_id=1, source_target_pairs={{0,1},{1,0},{2,3},{3,2},{4,5},{5,4},{6,7},{7,6},{8,9},{9,8},{10,11... | collective-permute-start | bytes 208904 | tf_op jit(solution)/shard_map/ppermute | solution.py:326
  5.8 1.5 %collective-permute-start.2 = (f32[136,128]{1,0:T(8,128)S(1)}, f32[136,128]{1,0:T(8,128)S(1)}, u32[]{:S(2)}, u32[]{:S(2)}) collective-permute-start(f32[136,128]{1,0:T(8,128)S(1)} %get-tuple-element.21), channel_id=1, source_target_pairs={{0,2},{1,3},{2,0},{3,1},{4,6},{5,7},{6,4},{7,5},{8,10},{9,11},{10,... | collective-permute-start | bytes 208904 | tf_op jit(solution)/shard_map/ppermute | solution.py:326
  7.3 0.0 collective-permute-start.3
  7.3 0.9 %collective-permute-done.1.refs_1_ = f32[136,128]{1,0:T(8,128)S(1)} collective-permute-done((f32[136,128]{1,0:T(8,128)S(1)}, f32[136,128]{1,0:T(8,128)S(1)}, u32[]{:S(2)}, u32[]{:S(2)}) %collective-permute-start.1) | collective-permute-done | bytes 69664 | tf_op jit(solution)/shard_map/ppermute | solution.py:326
  8.3 1.8 %collective-permute-done.2.refs_2_ = f32[136,128]{1,0:T(8,128)S(1)} collective-permute-done((f32[136,128]{1,0:T(8,128)S(1)}, f32[136,128]{1,0:T(8,128)S(1)}, u32[]{:S(2)}, u32[]{:S(2)}) %collective-permute-start.2) | collective-permute-done | bytes 69664 | tf_op jit(solution)/shard_map/ppermute | solution.py:326
  10.1 2.4 %collective-permute-done.3.refs_3_ = f32[136,128]{1,0:T(8,128)S(1)} collective-permute-done((f32[136,128]{1,0:T(8,128)S(1)}, f32[136,128]{1,0:T(8,128)S(1)}, u32[]{:S(2)}, u32[]{:S(2)}) %collective-permute-start.3) | collective-permute-done | bytes 69664 | tf_op jit(solution)/shard_map/ppermute | solution.py:326
  12.6 3.7 %collective-permute-start.6 = (f32[136,128]{1,0:T(8,128)S(1)}, f32[136,128]{1,0:T(8,128)S(1)}, u32[]{:S(2)}, u32[]{:S(2)}) collective-permute-start(f32[136,128]{1,0:T(8,128)S(1)} %shard_map.30.refs_0_), channel_id=1, source_target_pairs={{0,12},{1,13},{2,14},{3,15},{4,8},{5,9},{6,10},{7,11},{8,4},{9,5},... | collective-permute-start | bytes 208904 | tf_op jit(solution)/shard_map/ppermute | solution.py:326
  16.2 0.0 collective-permute-start.5
  16.2 0.8 %collective-permute-start.4 = (f32[136,128]{1,0:T(8,128)S(1)}, f32[136,128]{1,0:T(8,128)S(1)}, u32[]{:S(2)}, u32[]{:S(2)}) collective-permute-start(f32[136,128]{1,0:T(8,128)S(1)} %shard_map.30.refs_0_), channel_id=1, source_target_pairs={{0,4},{1,5},{2,6},{3,7},{4,0},{5,1},{6,2},{7,3},{8,12},{9,13},{10,... | collective-permute-start | bytes 208904 | tf_op jit(solution)/shard_map/ppermute | solution.py:326
  17.0 1.7 %collective-permute-done.6.refs_3_ = f32[136,128]{1,0:T(8,128)S(1)} collective-permute-done((f32[136,128]{1,0:T(8,128)S(1)}, f32[136,128]{1,0:T(8,128)S(1)}, u32[]{:S(2)}, u32[]{:S(2)}) %collective-permute-start.6) | collective-permute-done | bytes 69664 | tf_op jit(solution)/shard_map/ppermute | solution.py:326
  18.7 2.7 %collective-permute-done.5.refs_2_ = f32[136,128]{1,0:T(8,128)S(1)} collective-permute-done((f32[136,128]{1,0:T(8,128)S(1)}, f32[136,128]{1,0:T(8,128)S(1)}, u32[]{:S(2)}, u32[]{:S(2)}) %collective-permute-start.5) | collective-permute-done | bytes 69664 | tf_op jit(solution)/shard_map/ppermute | solution.py:326
  21.4 0.0 collective-permute-done.4.refs_1_
  21.5 0.6 %collective-permute-start.9 = (f32[136,128]{1,0:T(8,128)S(1)}, f32[136,128]{1,0:T(8,128)S(1)}, u32[]{:S(2)}, u32[]{:S(2)}) collective-permute-start(f32[136,128]{1,0:T(8,128)S(1)} %shard_map.31.refs_0_), channel_id=1, source_target_pairs={{0,3},{1,2},{2,1},{3,0},{4,7},{5,6},{6,5},{7,4},{8,11},{9,10},{10,... | collective-permute-start | bytes 208904 | tf_op jit(solution)/shard_map/ppermute | solution.py:326
  22.1 1.5 %collective-permute-start.8 = (f32[136,128]{1,0:T(8,128)S(1)}, f32[136,128]{1,0:T(8,128)S(1)}, u32[]{:S(2)}, u32[]{:S(2)}) collective-permute-start(f32[136,128]{1,0:T(8,128)S(1)} %shard_map.31.refs_0_), channel_id=1, source_target_pairs={{0,2},{1,3},{2,0},{3,1},{4,6},{5,7},{6,4},{7,5},{8,10},{9,11},{10,... | collective-permute-start | bytes 208904 | tf_op jit(solution)/shard_map/ppermute | solution.py:326
  23.6 1.4 %collective-permute-start.7 = (f32[136,128]{1,0:T(8,128)S(1)}, f32[136,128]{1,0:T(8,128)S(1)}, u32[]{:S(2)}, u32[]{:S(2)}) collective-permute-start(f32[136,128]{1,0:T(8,128)S(1)} %shard_map.31.refs_0_), channel_id=1, source_target_pairs={{0,1},{1,0},{2,3},{3,2},{4,5},{5,4},{6,7},{7,6},{8,9},{9,8},{10,11... | collective-permute-start | bytes 208904 | tf_op jit(solution)/shard_map/ppermute | solution.py:326
  25.0 0.0 collective-permute-start.10
  25.0 1.8 %collective-permute-done.9.refs_3_ = f32[136,128]{1,0:T(8,128)S(1)} collective-permute-done((f32[136,128]{1,0:T(8,128)S(1)}, f32[136,128]{1,0:T(8,128)S(1)}, u32[]{:S(2)}, u32[]{:S(2)}) %collective-permute-start.9) | collective-permute-done | bytes 69664 | tf_op jit(solution)/shard_map/ppermute | solution.py:326
  26.8 0.0 collective-permute-start.13
  26.8 0.3 collective-permute-done.8.refs_2_
  27.2 0.2 collective-permute-start.12
  27.4 0.5 %collective-permute-done.7.refs_1_ = f32[136,128]{1,0:T(8,128)S(1)} collective-permute-done((f32[136,128]{1,0:T(8,128)S(1)}, f32[136,128]{1,0:T(8,128)S(1)}, u32[]{:S(2)}, u32[]{:S(2)}) %collective-permute-start.7) | collective-permute-done | bytes 69664 | tf_op jit(solution)/shard_map/ppermute | solution.py:326
  27.9 0.0 collective-permute-start.11
  27.9 0.0 collective-permute-done.10.refs_4_
  27.9 0.2 collective-permute-done.13.refs_7_
  28.1 0.3 collective-permute-done.12.refs_6_
  28.4 0.7 %collective-permute-done.11.refs_5_ = f32[136,128]{1,0:T(8,128)S(1)} collective-permute-done((f32[136,128]{1,0:T(8,128)S(1)}, f32[136,128]{1,0:T(8,128)S(1)}, u32[]{:S(2)}, u32[]{:S(2)}) %collective-permute-start.11) | collective-permute-done | bytes 69664 | tf_op jit(solution)/shard_map/ppermute | solution.py:330
  29.1 8.7 %shard_map.32 = f32[512,256]{1,0:T(8,128)} custom-call(s32[3]{0:T(128)} %shifts.1, f32[136,128]{1,0:T(8,128)S(1)} %shard_map.31.refs_0_, f32[136,128]{1,0:T(8,128)S(1)} %collective-permute-done.7.refs_1_, f32[136,128]{1,0:T(8,128)S(1)} %collective-permute-done.8.refs_2_, f32[136,128]{1,0:T(8,128)S(1)} %collective-permute-done.9.refs_3_, ...), custom_call_target="tpu_custom_call" | custom-call | tf_op jit(solution)/shard_map/pallas_call | solution.py:361
  (2 shorter events, 0.1 us)
Async XLA Ops:
  0.0 2.2 %collective-permute-start = (f32[512,256]{1,0:T(8,128)}, f32[512,256]{1,0:T(8,128)S(1)}, u32[]{:S(2)}, u32[]{:S(2)}) collective-permute-start(f32[512,256]{1,0:T(8,128)} %own.1), channel_id=1, source_target_pairs={{0,16},{16,0},{1,17},{17,1},{2,18},{18,2},{3,19},{19,3},{4,20},{20... | collective-permute-start | bytes 1572872 | tf_op jit(solution)/shard_map/ppermute | solution.py:330
  2.9 5.4 %collective-permute-start.1 = (f32[136,128]{1,0:T(8,128)S(1)}, f32[136,128]{1,0:T(8,128)S(1)}, u32[]{:S(2)}, u32[]{:S(2)}) collective-permute-start(f32[136,128]{1,0:T(8,128)S(1)} %get-tuple-element.20), channel_id=1, source_target_pairs={{0,1},{1,0},{2,3},{3,2},{4,5},{5,4},{6,7},{7,6},{8,9},{9,8},{10,11... | collective-permute-start | bytes 208904 | tf_op jit(solution)/shard_map/ppermute | solution.py:326
  5.8 4.3 %collective-permute-start.2 = (f32[136,128]{1,0:T(8,128)S(1)}, f32[136,128]{1,0:T(8,128)S(1)}, u32[]{:S(2)}, u32[]{:S(2)}) collective-permute-start(f32[136,128]{1,0:T(8,128)S(1)} %get-tuple-element.21), channel_id=1, source_target_pairs={{0,2},{1,3},{2,0},{3,1},{4,6},{5,7},{6,4},{7,5},{8,10},{9,11},{10,... | collective-permute-start | bytes 208904 | tf_op jit(solution)/shard_map/ppermute | solution.py:326
  7.3 5.2 %collective-permute-start.3 = (f32[136,128]{1,0:T(8,128)S(1)}, f32[136,128]{1,0:T(8,128)S(1)}, u32[]{:S(2)}, u32[]{:S(2)}) collective-permute-start(f32[136,128]{1,0:T(8,128)S(1)} %get-tuple-element.22), channel_id=1, source_target_pairs={{0,3},{1,2},{2,1},{3,0},{4,7},{5,6},{6,5},{7,4},{8,11},{9,10},{10,... | collective-permute-start | bytes 208904 | tf_op jit(solution)/shard_map/ppermute | solution.py:326
  12.6 6.2 %collective-permute-start.6 = (f32[136,128]{1,0:T(8,128)S(1)}, f32[136,128]{1,0:T(8,128)S(1)}, u32[]{:S(2)}, u32[]{:S(2)}) collective-permute-start(f32[136,128]{1,0:T(8,128)S(1)} %shard_map.30.refs_0_), channel_id=1, source_target_pairs={{0,12},{1,13},{2,14},{3,15},{4,8},{5,9},{6,10},{7,11},{8,4},{9,5},... | collective-permute-start | bytes 208904 | tf_op jit(solution)/shard_map/ppermute | solution.py:326
  16.2 5.2 %collective-permute-start.5 = (f32[136,128]{1,0:T(8,128)S(1)}, f32[136,128]{1,0:T(8,128)S(1)}, u32[]{:S(2)}, u32[]{:S(2)}) collective-permute-start(f32[136,128]{1,0:T(8,128)S(1)} %shard_map.30.refs_0_), channel_id=1, source_target_pairs={{0,8},{1,9},{2,10},{3,11},{4,12},{5,13},{6,14},{7,15},{8,0},{9,1},... | collective-permute-start | bytes 208904 | tf_op jit(solution)/shard_map/ppermute | solution.py:326
  16.2 5.2 %collective-permute-start.4 = (f32[136,128]{1,0:T(8,128)S(1)}, f32[136,128]{1,0:T(8,128)S(1)}, u32[]{:S(2)}, u32[]{:S(2)}) collective-permute-start(f32[136,128]{1,0:T(8,128)S(1)} %shard_map.30.refs_0_), channel_id=1, source_target_pairs={{0,4},{1,5},{2,6},{3,7},{4,0},{5,1},{6,2},{7,3},{8,12},{9,13},{10,... | collective-permute-start | bytes 208904 | tf_op jit(solution)/shard_map/ppermute | solution.py:326
  21.5 5.4 %collective-permute-start.9 = (f32[136,128]{1,0:T(8,128)S(1)}, f32[136,128]{1,0:T(8,128)S(1)}, u32[]{:S(2)}, u32[]{:S(2)}) collective-permute-start(f32[136,128]{1,0:T(8,128)S(1)} %shard_map.31.refs_0_), channel_id=1, source_target_pairs={{0,3},{1,2},{2,1},{3,0},{4,7},{5,6},{6,5},{7,4},{8,11},{9,10},{10,... | collective-permute-start | bytes 208904 | tf_op jit(solution)/shard_map/ppermute | solution.py:326
  22.1 5.1 %collective-permute-start.8 = (f32[136,128]{1,0:T(8,128)S(1)}, f32[136,128]{1,0:T(8,128)S(1)}, u32[]{:S(2)}, u32[]{:S(2)}) collective-permute-start(f32[136,128]{1,0:T(8,128)S(1)} %shard_map.31.refs_0_), channel_id=1, source_target_pairs={{0,2},{1,3},{2,0},{3,1},{4,6},{5,7},{6,4},{7,5},{8,10},{9,11},{10,... | collective-permute-start | bytes 208904 | tf_op jit(solution)/shard_map/ppermute | solution.py:326
  23.6 4.3 %collective-permute-start.7 = (f32[136,128]{1,0:T(8,128)S(1)}, f32[136,128]{1,0:T(8,128)S(1)}, u32[]{:S(2)}, u32[]{:S(2)}) collective-permute-start(f32[136,128]{1,0:T(8,128)S(1)} %shard_map.31.refs_0_), channel_id=1, source_target_pairs={{0,1},{1,0},{2,3},{3,2},{4,5},{5,4},{6,7},{7,6},{8,9},{9,8},{10,11... | collective-permute-start | bytes 208904 | tf_op jit(solution)/shard_map/ppermute | solution.py:326
  25.0 2.9 %collective-permute-start.10 = (f32[136,128]{1,0:T(8,128)S(1)}, f32[136,128]{1,0:T(8,128)S(1)}, u32[]{:S(2)}, u32[]{:S(2)}) collective-permute-start(f32[136,128]{1,0:T(8,128)S(1)} %shard_map.31.refs_0_), channel_id=1, source_target_pairs={{0,16},{16,0},{1,17},{17,1},{2,18},{18,2},{3,19},{19,3},{4,20},{20... | collective-permute-start | bytes 208904 | tf_op jit(solution)/shard_map/ppermute | solution.py:330
  26.8 1.3 %collective-permute-start.13 = (f32[136,128]{1,0:T(8,128)S(1)}, f32[136,128]{1,0:T(8,128)S(1)}, u32[]{:S(2)}, u32[]{:S(2)}) collective-permute-start(f32[136,128]{1,0:T(8,128)S(1)} %collective-permute-done.9.refs_3_), channel_id=1, source_target_pairs={{0,16},{16,0},{1,17},{17,1},{2,18},{18,2},{3,19},{19,3},{4,20},{20... | collective-permute-start | bytes 208904 | tf_op jit(solution)/shard_map/ppermute | solution.py:330
  27.2 1.3 %collective-permute-start.12 = (f32[136,128]{1,0:T(8,128)S(1)}, f32[136,128]{1,0:T(8,128)S(1)}, u32[]{:S(2)}, u32[]{:S(2)}) collective-permute-start(f32[136,128]{1,0:T(8,128)S(1)} %collective-permute-done.8.refs_2_), channel_id=1, source_target_pairs={{0,16},{16,0},{1,17},{17,1},{2,18},{18,2},{3,19},{19,3},{4,20},{20... | collective-permute-start | bytes 208904 | tf_op jit(solution)/shard_map/ppermute | solution.py:330
  27.9 1.3 %collective-permute-start.11 = (f32[136,128]{1,0:T(8,128)S(1)}, f32[136,128]{1,0:T(8,128)S(1)}, u32[]{:S(2)}, u32[]{:S(2)}) collective-permute-start(f32[136,128]{1,0:T(8,128)S(1)} %collective-permute-done.7.refs_1_), channel_id=1, source_target_pairs={{0,16},{16,0},{1,17},{17,1},{2,18},{18,2},{3,19},{19,3},{4,20},{20... | collective-permute-start | bytes 208904 | tf_op jit(solution)/shard_map/ppermute | solution.py:330

commit v5 on v4

--- a/solution.py
+++ b/solution.py
@@ -286,7 +286,7 @@
         zero, one, between = each(
             lambda turn, parts: dots(turn, parts, 0),
             [turns[0], turns[1], turns[0]],
-            each(functools.partial(split, parts=3), right),
+            each(functools.partial(split, parts=2 if step else 3), right),
         )
         if step == 0:
             fetch.wait()

time: 38 us -> 37.8 us (level)
  no operation moved by 1% of the time
where the time goes in v5:
time: 37.8 us; the launch traced here: 37.7 us
  waiting for transfers between devices  13.6 us (36%)
  starting transfers between devices  13.1 us (35%)
  Pallas kernels  10.9 us (29%)
    ppermute x9, starting transfers between devices, across(): return lax.ppermute(x, 'rows', [(i, i ^ mask) for i in range(size)])  12.5 us
    ppermute x9, waiting for transfers between devices, across(): return lax.ppermute(x, 'rows', [(i, i ^ mask) for i in range(size)])  12.3 us
    pallas_call x1, Pallas kernels, one_sum(): kernel_of(rounds_kernel, jax.ShapeDtypeStruct((rows, width), F32), [HBM]...  8.53 us
    pallas_call x1, Pallas kernels, one_sum(): kernel_of(own_kernel, [part, part, part, square], [HBM], [pltpu.VMEM(matr...  1.68 us
    ppermute x5, waiting for transfers between devices, swapped(): return lax.ppermute(x, 'pos', [(0, 1), (1, 0)])  1.31 us
  transfers between devices with their start and end apart: 14, of which 12 were waited for; matrix products, arithmetic and copies ran while one was open for 0% of the time, Pallas kernels for 4%

profile of v5, /device:TPU:0, one launch (start us, length us, event | category | flops | bytes accessed | tf_op | source)
XLA Modules:
  0.0 37.7 jit_solution(12722344964233948634)
XLA Ops:
  0.0 0.5 %collective-permute-start = (f32[512,256]{1,0:T(8,128)}, f32[512,256]{1,0:T(8,128)S(1)}, u32[]{:S(2)}, u32[]{:S(2)}) collective-permute-start(f32[512,256]{1,0:T(8,128)} %own.1), channel_id=1, source_target_pairs={{0,16},{16,0},{1,17},{17,1},{2,18},{18,2},{3,19},{19,3},{4,20},{20... | collective-permute-start | bytes 1572872 | tf_op jit(solution)/shard_map/ppermute | solution.py:330
  0.5 1.7 %shard_map.28 = (bf16[512,256]{1,0:T(8,128)(2,1)S(1)}, bf16[512,256]{1,0:T(8,128)(2,1)S(1)}, bf16[512,256]{1,0:T(8,128)(2,1)S(1)}, f32[256,256]{1,0:T(8,128)S(1)}) custom-call(f32[512,256]{1,0:T(8,128)} %own.1), custom_call_target="tpu_custom_call" | custom-call | tf_op jit(solution)/shard_map/pallas_call | solution.py:341
  2.1 0.1 collective-permute-done.other
  2.2 0.7 %shard_map.29 = (f32[136,128]{1,0:T(8,128)S(1)}, f32[136,128]{1,0:T(8,128)S(1)}, f32[136,128]{1,0:T(8,128)S(1)}, f32[136,128]{1,0:T(8,128)S(1)}, bf16[512,256]{1...) custom-call(f32[512,256]{1,0:T(8,128)S(1)} %collective-permute-done.other, ...), custom_call_target="tpu_custom_call" | custom-call | tf_op jit(solution)/shard_map/pallas_call | solution.py:347
  2.9 2.9 %collective-permute-start.1 = (f32[136,128]{1,0:T(8,128)S(1)}, f32[136,128]{1,0:T(8,128)S(1)}, u32[]{:S(2)}, u32[]{:S(2)}) collective-permute-start(f32[136,128]{1,0:T(8,128)S(1)} %get-tuple-element.20), channel_id=1, source_target_pairs={{0,1},{1,0},{2,3},{3,2},{4,5},{5,4},{6,7},{7,6},{8,9},{9,8},{10,11... | collective-permute-start | bytes 208904 | tf_op jit(solution)/shard_map/ppermute | solution.py:326
  5.8 1.5 %collective-permute-start.2 = (f32[136,128]{1,0:T(8,128)S(1)}, f32[136,128]{1,0:T(8,128)S(1)}, u32[]{:S(2)}, u32[]{:S(2)}) collective-permute-start(f32[136,128]{1,0:T(8,128)S(1)} %get-tuple-element.21), channel_id=1, source_target_pairs={{0,2},{1,3},{2,0},{3,1},{4,6},{5,7},{6,4},{7,5},{8,10},{9,11},{10,... | collective-permute-start | bytes 208904 | tf_op jit(solution)/shard_map/ppermute | solution.py:326
  7.3 0.0 collective-permute-start.3
  7.3 0.9 %collective-permute-done.1.refs_1_ = f32[136,128]{1,0:T(8,128)S(1)} collective-permute-done((f32[136,128]{1,0:T(8,128)S(1)}, f32[136,128]{1,0:T(8,128)S(1)}, u32[]{:S(2)}, u32[]{:S(2)}) %collective-permute-start.1) | collective-permute-done | bytes 69664 | tf_op jit(solution)/shard_map/ppermute | solution.py:326
  8.3 1.8 %collective-permute-done.2.refs_2_ = f32[136,128]{1,0:T(8,128)S(1)} collective-permute-done((f32[136,128]{1,0:T(8,128)S(1)}, f32[136,128]{1,0:T(8,128)S(1)}, u32[]{:S(2)}, u32[]{:S(2)}) %collective-permute-start.2) | collective-permute-done | bytes 69664 | tf_op jit(solution)/shard_map/ppermute | solution.py:326
  10.1 2.4 %collective-permute-done.3.refs_3_ = f32[136,128]{1,0:T(8,128)S(1)} collective-permute-done((f32[136,128]{1,0:T(8,128)S(1)}, f32[136,128]{1,0:T(8,128)S(1)}, u32[]{:S(2)}, u32[]{:S(2)}) %collective-permute-start.3) | collective-permute-done | bytes 69664 | tf_op jit(solution)/shard_map/ppermute | solution.py:326
  12.6 3.7 %collective-permute-start.6 = (f32[136,128]{1,0:T(8,128)S(1)}, f32[136,128]{1,0:T(8,128)S(1)}, u32[]{:S(2)}, u32[]{:S(2)}) collective-permute-start(f32[136,128]{1,0:T(8,128)S(1)} %shard_map.30.refs_0_), channel_id=1, source_target_pairs={{0,12},{1,13},{2,14},{3,15},{4,8},{5,9},{6,10},{7,11},{8,4},{9,5},... | collective-permute-start | bytes 208904 | tf_op jit(solution)/shard_map/ppermute | solution.py:326
  16.2 0.0 collective-permute-start.5
  16.2 0.8 %collective-permute-start.4 = (f32[136,128]{1,0:T(8,128)S(1)}, f32[136,128]{1,0:T(8,128)S(1)}, u32[]{:S(2)}, u32[]{:S(2)}) collective-permute-start(f32[136,128]{1,0:T(8,128)S(1)} %shard_map.30.refs_0_), channel_id=1, source_target_pairs={{0,4},{1,5},{2,6},{3,7},{4,0},{5,1},{6,2},{7,3},{8,12},{9,13},{10,... | collective-permute-start | bytes 208904 | tf_op jit(solution)/shard_map/ppermute | solution.py:326
  17.0 1.7 %collective-permute-done.6.refs_3_ = f32[136,128]{1,0:T(8,128)S(1)} collective-permute-done((f32[136,128]{1,0:T(8,128)S(1)}, f32[136,128]{1,0:T(8,128)S(1)}, u32[]{:S(2)}, u32[]{:S(2)}) %collective-permute-start.6) | collective-permute-done | bytes 69664 | tf_op jit(solution)/shard_map/ppermute | solution.py:326
  18.7 2.7 %collective-permute-done.5.refs_2_ = f32[136,128]{1,0:T(8,128)S(1)} collective-permute-done((f32[136,128]{1,0:T(8,128)S(1)}, f32[136,128]{1,0:T(8,128)S(1)}, u32[]{:S(2)}, u32[]{:S(2)}) %collective-permute-start.5) | collective-permute-done | bytes 69664 | tf_op jit(solution)/shard_map/ppermute | solution.py:326
  21.4 0.0 collective-permute-done.4.refs_1_
  21.5 0.6 %collective-permute-start.9 = (f32[136,128]{1,0:T(8,128)S(1)}, f32[136,128]{1,0:T(8,128)S(1)}, u32[]{:S(2)}, u32[]{:S(2)}) collective-permute-start(f32[136,128]{1,0:T(8,128)S(1)} %shard_map.31.refs_0_), channel_id=1, source_target_pairs={{0,3},{1,2},{2,1},{3,0},{4,7},{5,6},{6,5},{7,4},{8,11},{9,10},{10,... | collective-permute-start | bytes 208904 | tf_op jit(solution)/shard_map/ppermute | solution.py:326
  22.1 1.5 %collective-permute-start.8 = (f32[136,128]{1,0:T(8,128)S(1)}, f32[136,128]{1,0:T(8,128)S(1)}, u32[]{:S(2)}, u32[]{:S(2)}) collective-permute-start(f32[136,128]{1,0:T(8,128)S(1)} %shard_map.31.refs_0_), channel_id=1, source_target_pairs={{0,2},{1,3},{2,0},{3,1},{4,6},{5,7},{6,4},{7,5},{8,10},{9,11},{10,... | collective-permute-start | bytes 208904 | tf_op jit(solution)/shard_map/ppermute | solution.py:326
  23.6 1.4 %collective-permute-start.7 = (f32[136,128]{1,0:T(8,128)S(1)}, f32[136,128]{1,0:T(8,128)S(1)}, u32[]{:S(2)}, u32[]{:S(2)}) collective-permute-start(f32[136,128]{1,0:T(8,128)S(1)} %shard_map.31.refs_0_), channel_id=1, source_target_pairs={{0,1},{1,0},{2,3},{3,2},{4,5},{5,4},{6,7},{7,6},{8,9},{9,8},{10,11... | collective-permute-start | bytes 208904 | tf_op jit(solution)/shard_map/ppermute | solution.py:326
  25.0 0.0 collective-permute-start.10
  25.0 1.8 %collective-permute-done.9.refs_3_ = f32[136,128]{1,0:T(8,128)S(1)} collective-permute-done((f32[136,128]{1,0:T(8,128)S(1)}, f32[136,128]{1,0:T(8,128)S(1)}, u32[]{:S(2)}, u32[]{:S(2)}) %collective-permute-start.9) | collective-permute-done | bytes 69664 | tf_op jit(solution)/shard_map/ppermute | solution.py:326
  26.8 0.0 collective-permute-start.13
  26.8 0.3 collective-permute-done.8.refs_2_
  27.2 0.2 collective-permute-start.12
  27.4 0.5 %collective-permute-done.7.refs_1_ = f32[136,128]{1,0:T(8,128)S(1)} collective-permute-done((f32[136,128]{1,0:T(8,128)S(1)}, f32[136,128]{1,0:T(8,128)S(1)}, u32[]{:S(2)}, u32[]{:S(2)}) %collective-permute-start.7) | collective-permute-done | bytes 69664 | tf_op jit(solution)/shard_map/ppermute | solution.py:326
  27.9 0.0 collective-permute-start.11
  27.9 0.0 collective-permute-done.10.refs_4_
  27.9 0.2 collective-permute-done.13.refs_7_
  28.1 0.3 collective-permute-done.12.refs_6_
  28.4 0.7 %collective-permute-done.11.refs_5_ = f32[136,128]{1,0:T(8,128)S(1)} collective-permute-done((f32[136,128]{1,0:T(8,128)S(1)}, f32[136,128]{1,0:T(8,128)S(1)}, u32[]{:S(2)}, u32[]{:S(2)}) %collective-permute-start.11) | collective-permute-done | bytes 69664 | tf_op jit(solution)/shard_map/ppermute | solution.py:330
  29.1 8.5 %shard_map.32 = f32[512,256]{1,0:T(8,128)} custom-call(s32[3]{0:T(128)} %shifts.1, f32[136,128]{1,0:T(8,128)S(1)} %shard_map.31.refs_0_, f32[136,128]{1,0:T(8,128)S(1)} %collective-permute-done.7.refs_1_, f32[136,128]{1,0:T(8,128)S(1)} %collective-permute-done.8.refs_2_, f32[136,128]{1,0:T(8,128)S(1)} %collective-permute-done.9.refs_3_, ...), custom_call_target="tpu_custom_call" | custom-call | tf_op jit(solution)/shard_map/pallas_call | solution.py:361
  (2 shorter events, 0.1 us)
Async XLA Ops:
  0.0 2.2 %collective-permute-start = (f32[512,256]{1,0:T(8,128)}, f32[512,256]{1,0:T(8,128)S(1)}, u32[]{:S(2)}, u32[]{:S(2)}) collective-permute-start(f32[512,256]{1,0:T(8,128)} %own.1), channel_id=1, source_target_pairs={{0,16},{16,0},{1,17},{17,1},{2,18},{18,2},{3,19},{19,3},{4,20},{20... | collective-permute-start | bytes 1572872 | tf_op jit(solution)/shard_map/ppermute | solution.py:330
  2.9 5.4 %collective-permute-start.1 = (f32[136,128]{1,0:T(8,128)S(1)}, f32[136,128]{1,0:T(8,128)S(1)}, u32[]{:S(2)}, u32[]{:S(2)}) collective-permute-start(f32[136,128]{1,0:T(8,128)S(1)} %get-tuple-element.20), channel_id=1, source_target_pairs={{0,1},{1,0},{2,3},{3,2},{4,5},{5,4},{6,7},{7,6},{8,9},{9,8},{10,11... | collective-permute-start | bytes 208904 | tf_op jit(solution)/shard_map/ppermute | solution.py:326
  5.8 4.3 %collective-permute-start.2 = (f32[136,128]{1,0:T(8,128)S(1)}, f32[136,128]{1,0:T(8,128)S(1)}, u32[]{:S(2)}, u32[]{:S(2)}) collective-permute-start(f32[136,128]{1,0:T(8,128)S(1)} %get-tuple-element.21), channel_id=1, source_target_pairs={{0,2},{1,3},{2,0},{3,1},{4,6},{5,7},{6,4},{7,5},{8,10},{9,11},{10,... | collective-permute-start | bytes 208904 | tf_op jit(solution)/shard_map/ppermute | solution.py:326
  7.3 5.2 %collective-permute-start.3 = (f32[136,128]{1,0:T(8,128)S(1)}, f32[136,128]{1,0:T(8,128)S(1)}, u32[]{:S(2)}, u32[]{:S(2)}) collective-permute-start(f32[136,128]{1,0:T(8,128)S(1)} %get-tuple-element.22), channel_id=1, source_target_pairs={{0,3},{1,2},{2,1},{3,0},{4,7},{5,6},{6,5},{7,4},{8,11},{9,10},{10,... | collective-permute-start | bytes 208904 | tf_op jit(solution)/shard_map/ppermute | solution.py:326
  12.6 6.2 %collective-permute-start.6 = (f32[136,128]{1,0:T(8,128)S(1)}, f32[136,128]{1,0:T(8,128)S(1)}, u32[]{:S(2)}, u32[]{:S(2)}) collective-permute-start(f32[136,128]{1,0:T(8,128)S(1)} %shard_map.30.refs_0_), channel_id=1, source_target_pairs={{0,12},{1,13},{2,14},{3,15},{4,8},{5,9},{6,10},{7,11},{8,4},{9,5},... | collective-permute-start | bytes 208904 | tf_op jit(solution)/shard_map/ppermute | solution.py:326
  16.2 5.2 %collective-permute-start.5 = (f32[136,128]{1,0:T(8,128)S(1)}, f32[136,128]{1,0:T(8,128)S(1)}, u32[]{:S(2)}, u32[]{:S(2)}) collective-permute-start(f32[136,128]{1,0:T(8,128)S(1)} %shard_map.30.refs_0_), channel_id=1, source_target_pairs={{0,8},{1,9},{2,10},{3,11},{4,12},{5,13},{6,14},{7,15},{8,0},{9,1},... | collective-permute-start | bytes 208904 | tf_op jit(solution)/shard_map/ppermute | solution.py:326
  16.2 5.2 %collective-permute-start.4 = (f32[136,128]{1,0:T(8,128)S(1)}, f32[136,128]{1,0:T(8,128)S(1)}, u32[]{:S(2)}, u32[]{:S(2)}) collective-permute-start(f32[136,128]{1,0:T(8,128)S(1)} %shard_map.30.refs_0_), channel_id=1, source_target_pairs={{0,4},{1,5},{2,6},{3,7},{4,0},{5,1},{6,2},{7,3},{8,12},{9,13},{10,... | collective-permute-start | bytes 208904 | tf_op jit(solution)/shard_map/ppermute | solution.py:326
  21.5 5.4 %collective-permute-start.9 = (f32[136,128]{1,0:T(8,128)S(1)}, f32[136,128]{1,0:T(8,128)S(1)}, u32[]{:S(2)}, u32[]{:S(2)}) collective-permute-start(f32[136,128]{1,0:T(8,128)S(1)} %shard_map.31.refs_0_), channel_id=1, source_target_pairs={{0,3},{1,2},{2,1},{3,0},{4,7},{5,6},{6,5},{7,4},{8,11},{9,10},{10,... | collective-permute-start | bytes 208904 | tf_op jit(solution)/shard_map/ppermute | solution.py:326
  22.1 5.1 %collective-permute-start.8 = (f32[136,128]{1,0:T(8,128)S(1)}, f32[136,128]{1,0:T(8,128)S(1)}, u32[]{:S(2)}, u32[]{:S(2)}) collective-permute-start(f32[136,128]{1,0:T(8,128)S(1)} %shard_map.31.refs_0_), channel_id=1, source_target_pairs={{0,2},{1,3},{2,0},{3,1},{4,6},{5,7},{6,4},{7,5},{8,10},{9,11},{10,... | collective-permute-start | bytes 208904 | tf_op jit(solution)/shard_map/ppermute | solution.py:326
  23.6 4.3 %collective-permute-start.7 = (f32[136,128]{1,0:T(8,128)S(1)}, f32[136,128]{1,0:T(8,128)S(1)}, u32[]{:S(2)}, u32[]{:S(2)}) collective-permute-start(f32[136,128]{1,0:T(8,128)S(1)} %shard_map.31.refs_0_), channel_id=1, source_target_pairs={{0,1},{1,0},{2,3},{3,2},{4,5},{5,4},{6,7},{7,6},{8,9},{9,8},{10,11... | collective-permute-start | bytes 208904 | tf_op jit(solution)/shard_map/ppermute | solution.py:326
  25.0 2.9 %collective-permute-start.10 = (f32[136,128]{1,0:T(8,128)S(1)}, f32[136,128]{1,0:T(8,128)S(1)}, u32[]{:S(2)}, u32[]{:S(2)}) collective-permute-start(f32[136,128]{1,0:T(8,128)S(1)} %shard_map.31.refs_0_), channel_id=1, source_target_pairs={{0,16},{16,0},{1,17},{17,1},{2,18},{18,2},{3,19},{19,3},{4,20},{20... | collective-permute-start | bytes 208904 | tf_op jit(solution)/shard_map/ppermute | solution.py:330
  26.8 1.3 %collective-permute-start.13 = (f32[136,128]{1,0:T(8,128)S(1)}, f32[136,128]{1,0:T(8,128)S(1)}, u32[]{:S(2)}, u32[]{:S(2)}) collective-permute-start(f32[136,128]{1,0:T(8,128)S(1)} %collective-permute-done.9.refs_3_), channel_id=1, source_target_pairs={{0,16},{16,0},{1,17},{17,1},{2,18},{18,2},{3,19},{19,3},{4,20},{20... | collective-permute-start | bytes 208904 | tf_op jit(solution)/shard_map/ppermute | solution.py:330
  27.2 1.3 %collective-permute-start.12 = (f32[136,128]{1,0:T(8,128)S(1)}, f32[136,128]{1,0:T(8,128)S(1)}, u32[]{:S(2)}, u32[]{:S(2)}) collective-permute-start(f32[136,128]{1,0:T(8,128)S(1)} %collective-permute-done.8.refs_2_), channel_id=1, source_target_pairs={{0,16},{16,0},{1,17},{17,1},{2,18},{18,2},{3,19},{19,3},{4,20},{20... | collective-permute-start | bytes 208904 | tf_op jit(solution)/shard_map/ppermute | solution.py:330
  27.9 1.3 %collective-permute-start.11 = (f32[136,128]{1,0:T(8,128)S(1)}, f32[136,128]{1,0:T(8,128)S(1)}, u32[]{:S(2)}, u32[]{:S(2)}) collective-permute-start(f32[136,128]{1,0:T(8,128)S(1)} %collective-permute-done.7.refs_1_), channel_id=1, source_target_pairs={{0,16},{16,0},{1,17},{17,1},{2,18},{18,2},{3,19},{19,3},{4,20},{20... | collective-permute-start | bytes 208904 | tf_op jit(solution)/shard_map/ppermute | solution.py:330
